TPU v7x, 32 devices: a whole 2x2x4 slice. The times are simulated.
32 devices in a mesh: fsdp: 32 (over z, y, x, core).
Axes of the slice: x: 2, y: 2, z: 4, core: 2. Of those that a mesh axis runs over, the one named last changes fastest.
Arguments:
- hidden_in: bfloat16 [32768, 768], P('fsdp'), may hold values from -6 to 6
- segment_ids: int32 [32768], P('fsdp'), may hold values from -1 to 543, as said below
- project_in: bfloat16 [2304, 768], P('fsdp'), may hold values from -0.21875 to 0.21875
- project_out: bfloat16 [768, 768], P('fsdp'), may hold values from -0.625 to 0.625
- expand_weight: bfloat16 [2304, 768], P('fsdp'), may hold values from -0.21875 to 0.21875
- shrink_weight: bfloat16 [768, 1152], P('fsdp'), may hold values from -0.1875 to 0.1875
- first_gain: bfloat16 [768], P('fsdp'), may hold values from 0.5 to 1.5
- second_gain: bfloat16 [768], P('fsdp'), may hold values from 0.5 to 1.5
- cotangent: bfloat16 [32768, 768], P('fsdp'), may hold values from -6 to 6
Outputs:
- hidden_out: bfloat16 [32768, 768], P('fsdp')
- grad_input: bfloat16 [32768, 768], P('fsdp')
- grad_project_in: float32 [2304, 768], P('fsdp')
- grad_project_out: float32 [768, 768], P('fsdp')
- grad_expand: float32 [2304, 768], P('fsdp')
- grad_shrink: float32 [768, 1152], P('fsdp')
- grad_first_gain: float32 [768], P('fsdp')
- grad_second_gain: float32 [768], P('fsdp')
Inputs may be any that keep to these rules, and one draw needn't show every extreme that they name: `segment_ids`: within each aligned block of 1024 slots, equal numbers form one run (one sequence of at most 512 tokens); -1 marks padding, which stands only at the end of a block; runs of different blocks carry different numbers. Some sequence has exactly 512 tokens, and some block has no padding.
All inputs are finite; a program needn't handle non-finite values.
Results may differ from a plain program's by a relative error of at most 0.01.
Values may be sent and summed in bfloat16 or wider, within the bound.
A program may use at most 320 MiB of HBM per device.

v0:
```python
import jax
import jax.numpy as jnp
from jax import lax
from jax.sharding import PartitionSpec as P

D = 768
HEADS = 12
HEAD_DIM = 64
FF = 1152


eps_norm = 1e-05
rope_base = 160000.0
masked_score = -1e30


def layer_norm(values, gain):
    center = jnp.mean(values, axis=-1, keepdims=True)
    centred = values - center
    spread = jnp.mean(centred * centred, axis=-1, keepdims=True)
    return centred * lax.rsqrt(spread + eps_norm) * gain


def gated_gelu(gate, upward):
    return jax.nn.gelu(gate, approximate=False) * upward


def rotate_half(values):
    middle_index = values.shape[-1] // 2
    return jnp.concatenate([-values[..., middle_index:], values[..., :middle_index]], axis=-1)


def rope_tables(segment_ids, head_size):
    slot_count = segment_ids.shape[0]
    slots = jnp.arange(slot_count, dtype=jnp.int32)
    changed = jnp.concatenate([jnp.ones((1,), dtype=bool), segment_ids[1:] != segment_ids[:-1]])
    starts = lax.cummax(jnp.where(changed, slots, jnp.zeros_like(slots)), axis=0)
    position = (slots - starts).astype(jnp.float32)
    freq = rope_base ** (-jnp.arange(head_size // 2, dtype=jnp.float32) * 2.0 / head_size)
    angle = position[:, None] * freq[None, :]
    angle = jnp.concatenate([angle, angle], axis=-1)
    return (jnp.cos(angle), jnp.sin(angle))


def apply_rope(values, cosine, sine):
    return values * cosine[:, None, :] + rotate_half(values) * sine[:, None, :]


def undo_rope(grads, cosine, sine):
    return grads * cosine[:, None, :] - rotate_half(grads * sine[:, None, :])


def right_product(left, weight):
    return lax.dot_general(
        left, weight, (((1,), (1,)), ((), ())), preferred_element_type=jnp.float32
    )


def outer_sum(grads, inputs):
    return lax.dot_general(
        grads, inputs, (((0,), (0,)), ((), ())), preferred_element_type=jnp.float32
    )


def local(
    hidden_in,
    segment_ids,
    project_in,
    project_out,
    expand_weight,
    shrink_weight,
    first_gain,
    second_gain,
    cotangent,
):
    slot_count = hidden_in.shape[0]
    score_scale = HEAD_DIM ** (-0.5)
    block_rows = min(512, slot_count)
    gathered = (
        lax.all_gather(project_in, "fsdp", axis=0, tiled=True),
        lax.all_gather(project_out, "fsdp", axis=0, tiled=True),
        lax.all_gather(expand_weight, "fsdp", axis=0, tiled=True),
        lax.all_gather(shrink_weight, "fsdp", axis=0, tiled=True),
        lax.all_gather(first_gain, "fsdp", axis=0, tiled=True),
        lax.all_gather(second_gain, "fsdp", axis=0, tiled=True),
    )
    full_in, full_out, full_expand, full_shrink, gain_one, gain_two = gathered
    hidden = hidden_in.astype(jnp.float32)
    normed, norm_back_one = jax.vjp(layer_norm, hidden, gain_one.astype(jnp.float32))
    normed_low = normed.astype(jnp.bfloat16)
    joined = right_product(normed_low, full_in)
    cosine, sine = rope_tables(segment_ids, HEAD_DIM)
    queries_low = apply_rope(
        joined[:, :D].reshape(slot_count, HEADS, HEAD_DIM), cosine, sine
    ).astype(jnp.bfloat16)
    keys_low = apply_rope(
        joined[:, D : 2 * D].reshape(slot_count, HEADS, HEAD_DIM), cosine, sine
    ).astype(jnp.bfloat16)
    values_low = joined[:, 2 * D :].reshape(slot_count, HEADS, HEAD_DIM).astype(jnp.bfloat16)
    slots = jnp.arange(slot_count, dtype=jnp.int32)

    def block_scores(offset):
        seg_rows = segment_ids[offset : offset + block_rows]
        same_seq = (seg_rows[:, None] == segment_ids[None, :]) & (seg_rows[:, None] >= 0)
        allowed = same_seq | (slots[offset : offset + block_rows, None] == slots[None, :])
        raw = (
            jnp.einsum(
                "qhd,khd->hqk",
                queries_low[offset : offset + block_rows],
                keys_low,
                preferred_element_type=jnp.float32,
            )
            * score_scale
        )
        return jnp.where(allowed[None], raw, masked_score)

    mixed_parts = []
    lse_parts = []
    for number in range(slot_count // block_rows):
        offset = number * block_rows
        scores = block_scores(offset)
        row_peak = jnp.max(scores, axis=-1, keepdims=True)
        shifted = jnp.exp(scores - row_peak)
        row_total = jnp.sum(shifted, axis=-1, keepdims=True)
        probs_low = (shifted / row_total).astype(jnp.bfloat16)
        lse_parts.append(row_peak + jnp.log(row_total))
        mixed_parts.append(
            jnp.einsum("hqk,khd->qhd", probs_low, values_low, preferred_element_type=jnp.float32)
        )
    mixed_low = jnp.concatenate(mixed_parts, axis=0).reshape(slot_count, D).astype(jnp.bfloat16)
    middle = hidden + right_product(mixed_low, full_out)
    normed_two, norm_back_two = jax.vjp(layer_norm, middle, gain_two.astype(jnp.float32))
    normed_two_low = normed_two.astype(jnp.bfloat16)
    widened = right_product(normed_two_low, full_expand)
    product, glu_back = jax.vjp(gated_gelu, widened[:, :FF], widened[:, FF:])
    product_low = product.astype(jnp.bfloat16)
    hidden_out = (middle + right_product(product_low, full_shrink)).astype(jnp.bfloat16)
    back_in, back_out, back_expand, back_shrink = (
        lax.all_gather(project_in, "fsdp", axis=0, tiled=True),
        lax.all_gather(project_out, "fsdp", axis=0, tiled=True),
        lax.all_gather(expand_weight, "fsdp", axis=0, tiled=True),
        lax.all_gather(shrink_weight, "fsdp", axis=0, tiled=True),
    )
    grad_shrink = outer_sum(cotangent, product_low)
    grad_product = jnp.dot(cotangent, back_shrink, preferred_element_type=jnp.float32)
    grad_gate, grad_upward = glu_back(grad_product)
    grad_wide = jnp.concatenate([grad_gate, grad_upward], axis=1).astype(jnp.bfloat16)
    grad_expand = outer_sum(grad_wide, normed_two_low)
    grad_normed_two = jnp.dot(grad_wide, back_expand, preferred_element_type=jnp.float32)
    grad_mid_norm, grad_gain_two = norm_back_two(grad_normed_two)
    grad_middle = cotangent.astype(jnp.float32) + grad_mid_norm
    grad_mid_low = grad_middle.astype(jnp.bfloat16)
    grad_project_out = outer_sum(grad_mid_low, mixed_low)
    grad_mixed = (
        jnp.dot(grad_mid_low, back_out, preferred_element_type=jnp.float32)
        .astype(jnp.bfloat16)
        .reshape(slot_count, HEADS, HEAD_DIM)
    )
    grad_values = jnp.zeros((slot_count, HEADS, HEAD_DIM), jnp.float32)
    grad_keys = jnp.zeros((slot_count, HEADS, HEAD_DIM), jnp.float32)
    query_parts = []
    for number in range(slot_count // block_rows):
        offset = number * block_rows
        scores = block_scores(offset)
        probs = jnp.exp(scores - lse_parts[number])
        probs_low = probs.astype(jnp.bfloat16)
        grad_block = grad_mixed[offset : offset + block_rows]
        grad_values = grad_values + jnp.einsum(
            "hqk,qhd->khd", probs_low, grad_block, preferred_element_type=jnp.float32
        )
        grad_probs = jnp.einsum(
            "qhd,khd->hqk", grad_block, values_low, preferred_element_type=jnp.float32
        )
        row_dot = jnp.sum(probs * grad_probs, axis=-1, keepdims=True)
        grad_scores = (probs * (grad_probs - row_dot)).astype(jnp.bfloat16)
        query_parts.append(
            jnp.einsum("hqk,khd->qhd", grad_scores, keys_low, preferred_element_type=jnp.float32)
            * score_scale
        )
        grad_keys = (
            grad_keys
            + jnp.einsum(
                "hqk,qhd->khd",
                grad_scores,
                queries_low[offset : offset + block_rows],
                preferred_element_type=jnp.float32,
            )
            * score_scale
        )
    grad_queries = jnp.concatenate(query_parts, axis=0)
    grad_joined = jnp.concatenate(
        [
            undo_rope(grad_queries, cosine, sine).reshape(slot_count, D),
            undo_rope(grad_keys, cosine, sine).reshape(slot_count, D),
            grad_values.reshape(slot_count, D),
        ],
        axis=1,
    ).astype(jnp.bfloat16)
    grad_project_in = outer_sum(grad_joined, normed_low)
    grad_normed = jnp.dot(grad_joined, back_in, preferred_element_type=jnp.float32)
    grad_hidden_norm, grad_gain_one = norm_back_one(grad_normed)
    grad_input = (grad_middle + grad_hidden_norm).astype(jnp.bfloat16)
    owned_in, owned_out, owned_expand, owned_shrink, owned_gain_one, owned_gain_two = (
        lax.psum_scatter(grad_project_in, "fsdp", scatter_dimension=0, tiled=True),
        lax.psum_scatter(grad_project_out, "fsdp", scatter_dimension=0, tiled=True),
        lax.psum_scatter(grad_expand, "fsdp", scatter_dimension=0, tiled=True),
        lax.psum_scatter(grad_shrink, "fsdp", scatter_dimension=0, tiled=True),
        lax.psum_scatter(grad_gain_one, "fsdp", scatter_dimension=0, tiled=True),
        lax.psum_scatter(grad_gain_two, "fsdp", scatter_dimension=0, tiled=True),
    )
    return (
        hidden_out,
        grad_input,
        owned_in,
        owned_out,
        owned_expand,
        owned_shrink,
        owned_gain_one,
        owned_gain_two,
    )


def solution(mesh):
    return jax.shard_map(
        local,
        mesh=mesh,
        in_specs=(
            P("fsdp", None),
            P("fsdp"),
            P("fsdp", None),
            P("fsdp", None),
            P("fsdp", None),
            P("fsdp", None),
            P("fsdp"),
            P("fsdp"),
            P("fsdp", None),
        ),
        out_specs=(
            P("fsdp", None),
            P("fsdp", None),
            P("fsdp", None),
            P("fsdp", None),
            P("fsdp", None),
            P("fsdp", None),
            P("fsdp"),
            P("fsdp"),
        ),
        check_vma=False,
    )
```

profile of v0, /device:TPU:0, one launch (start us, length us, event | category | flops | bytes accessed | tf_op | source)
XLA Modules:
  0.0 773.3 jit_solution(16888591882348659515)
XLA Ops:
  14.1 42.2 %all-reduce.6 = (bf16[768]{0:T(1024)(128)(2,1)S(1)}, bf16[768]{0:T(1024)(128)(2,1)S(1)}) all-reduce(bf16[768]{0:T(1024)(128)(2,1)S(1)} %dynamic-update-slice, bf16[768]{0:T(1024)(128)(2,1)S(1)} %dynamic-update-slice.1), channel_id=1, replica_groups=mesh['fsdp'=32] {'fsdp'}, use_global_device_ids=true, to_apply=%add | all-reduce | flops 1536 | bytes 6144
  66.4 7.6 all-gather.5.cloned.1.call-done
  74.0 6.2 fusion.60
  89.8 3.6 copy.45
  100.1 10.8 %fusion.13 = (f32[12,512]{1,0:T(8,128)S(1)}, f32[12,512,1024]{2,1,0:T(8,128)}) fusion(pred[512,1024]{1,0:T(8,128)(4,1)S(1)} %copy-done.16, bf16[1024,12,64]{0,2,1:T(8,128)(2,1)S(1)} %get-tuple-element.59, bf16[1024,12,64]{0,2,1:T(8,128)(2,1)S(1)} %get-tuple-element.58), kind=kOutput, calls=%fused_computation.23 | convolution fusion | flops 824174592 | bytes 28073984 | tf_op jit(solution)/shard_map/qhd,khd->hqk/dot_general | solution.py:107
  110.9 10.7 %fusion.12 = (f32[12,512]{1,0:T(8,128)S(1)}, f32[12,512,1024]{2,1,0:T(8,128)}) fusion(pred[512,1024]{1,0:T(8,128)(4,1)S(1)} %copy-done.13, bf16[1024,12,64]{0,2,1:T(8,128)(2,1)S(1)} %get-tuple-element.59, bf16[1024,12,64]{0,2,1:T(8,128)(2,1)S(1)} %get-tuple-element.58), kind=kOutput, calls=%fused_computation.22 | convolution fusion | flops 824174592 | bytes 28073984 | tf_op jit(solution)/shard_map/qhd,khd->hqk/dot_general | solution.py:107
  121.7 11.8 %fusion.1 = f32[12,512]{1,0:T(8,128)S(1)} fusion(f32[12,512]{1,0:T(8,128)S(1)} %get-tuple-element.70, f32[12,512,1024]{2,1,0:T(8,128)} %get-tuple-element.71, pred[512,1024]{1,0:T(8,128)(4,1)S(1)} %copy-done.16), kind=kLoop, calls=%fused_computation.13 | loop fusion | flops 25159680 | bytes 25739264 | tf_op jit(solution)/shard_map/reduce_sum | solution.py:124
  133.6 13.8 %fusion.50 = bf16[512,12,64]{0,2,1:T(8,128)(2,1)} fusion(bf16[1024,12,64]{0,2,1:T(8,128)(2,1)S(1)} %bitcast.81, f32[12,512]{1,0:T(8,128)S(1)} %fusion.1, f32[12,512]{1,0:T(8,128)S(1)} %get-tuple-element.70, f32[12,512,1024]{2,1,0:T(8,128)} %get-tuple-element.71, pred[512,1024]{1,0:T(8,128)(4,1)S(1)} %copy-done.16), kind=kOutput, calls=%fused_computation.107 | convolution fusion | flops 837156864 | bytes 28098560 | tf_op jit(solution)/shard_map/hqk,khd->qhd/dot_general | solution.py:128
  149.3 7.3 fusion
  156.6 8.7 %fusion.49 = bf16[512,12,64]{0,2,1:T(8,128)(2,1)} fusion(bf16[1024,12,64]{0,2,1:T(8,128)(2,1)S(1)} %bitcast.82, f32[12,512]{1,0:T(8,128)S(1)} %fusion, f32[12,512]{1,0:T(8,128)S(1)} %get-tuple-element.72, f32[12,512,1024]{2,1,0:T(8,128)S(1)} %bitcast.74, pred[512,1024]{1,0:T(8,128)(4,1)S(1)} %copy-done.13), kind=kOutput, calls=%fused_computation.106 | convolution fusion | flops 837156864 | bytes 28098560 | tf_op jit(solution)/shard_map/hqk,khd->qhd/dot_general | solution.py:128
  173.0 18.7 %all-gather.9.cloned.1.call-done = bf16[2304,768]{1,0:T(8,128)(2,1)} async-done(((bf16[72,768]{1,0:T(8,128)(2,1)}), bf16[2304,768]{1,0:T(8,128)(2,1)}) %all-gather.9.cloned.1.call-update) | async-done | bytes 3538960 | tf_op jit(solution)/shard_map/all_gather | solution.py:82
  191.8 10.7 %fusion.79 = f32[1024,2304]{1,0:T(8,128)} fusion(bf16[2304,768]{1,0:T(8,128)(2,1)} %all-gather.9.cloned.1.call-done, f32[1024,768]{0,1:T(8,128)} %copy-done.19, f32[768]{0:T(1024)S(1)} %copy-done.55, f32[1024]{0:T(1024)S(1)} %fusion.66, f32[1024]{0:T(1024)S(1)} %broadcast_multiply_fusion.3), kind=kOutput, calls=%fused_computation.157 | convolution fusion | flops 3627024384 | bytes 16133120 | tf_op jit(solution)/shard_map/dot_general | solution.py:54
  202.5 46.4 %all-gather.11.cloned.1.call-done = bf16[768,1152]{1,0:T(8,128)(2,1)} async-done(((bf16[24,1152]{1,0:T(8,128)(2,1)}), bf16[768,1152]{1,0:T(8,128)(2,1)}) %all-gather.11.cloned.1.call-update) | async-done | bytes 1769488 | tf_op jit(solution)/shard_map/all_gather | solution.py:83
  248.9 16.1 %add_convert_fusion = (bf16[1024,1152]{1,0:T(8,128)(2,1)}, f32[1024,1152]{1,0:T(8,128)S(1)}, f32[1024,1152]{1,0:T(8,128)S(1)}) fusion(f32[1024,2304]{1,0:T(8,128)} %fusion.79, bf16[1024,768]{1,0:T(8,128)(2,1)S(1)} %copy-done.34, bf16[768,1152]{1,0:T(8,128)(2,1)} %all-gather.11.cloned.1.call-done), kind=kOutput, calls=%fused_computation.38 | convolution fusion | flops 1898053632 | bytes 24576000 | tf_op jit(solution)/shard_map/dot_general | solution.py:145
  269.2 3.9 convolution_bitcast_fusion
  273.2 9.8 %multiply_reduce_fusion.2 = (f32[768]{0:T(1024)}, f32[1024]{0:T(1024)S(1)}, f32[1024,768]{0,1:T(8,128)S(1)}) fusion(f32[1024,768]{0,1:T(8,128)} %copy-done.19, f32[1024]{0:T(1024)S(1)} %fusion.66, f32[1024]{0:T(1024)S(1)} %broadcast_multiply_fusion.3, f32[768]{0:T(1024)S(1)} %copy-done.55, bf16[2304,768]{1,0:T(8,128)(2,1)} %all-gather.9.cloned.1.call-done, ...), kind=kOutput, calls=%fused_computation.78 | convolution fusion | flops 3638819072 | bytes 14567424 | tf_op jit(solution)/shard_map/dot_general | solution.py:149
  293.5 7.3 fusion.38
  302.0 17.9 %multiply_reduce_fusion.1 = (f32[12,512]{1,0:T(8,128)S(1)}, f32[12,512,1024]{2,1,0:T(8,128)}) fusion(f32[12,512]{1,0:T(8,128)S(1)} %log_add_fusion.1, f32[12,512,1024]{2,1,0:T(8,128)} %get-tuple-element.73, pred[512,1024]{1,0:T(8,128)(4,1)S(1)} %copy-done.14, bf16[512,12,64]{0,2,1:T(8,128)(2,1)} %bitcast.89, bf16[1024,12,64]{0,2,1:T(8,128)(2,1)S(1)} %bitcast.83), kind=kOutput, calls=%fused_computation.4 | convolution fusion | flops 836757504 | bytes 53264384 | tf_op jit(solution)/shard_map/qhd,khd->hqk/dot_general | solution.py:171
  319.9 17.8 %multiply_reduce_fusion = (f32[12,512]{1,0:T(8,128)S(1)}, f32[12,512,1024]{2,1,0:T(8,128)}) fusion(f32[12,512]{1,0:T(8,128)S(1)} %log_add_fusion, f32[12,512,1024]{2,1,0:T(8,128)} %get-tuple-element.71, pred[512,1024]{1,0:T(8,128)(4,1)S(1)} %copy-done.17, bf16[512,12,64]{0,2,1:T(8,128)(2,1)} %bitcast.91, bf16[1024,12,64]{0,2,1:T(8,128)(2,1)S(1)} %bitcast.84), kind=kOutput, calls=%fused_computation.1 | convolution fusion | flops 836757504 | bytes 53264384 | tf_op jit(solution)/shard_map/qhd,khd->hqk/dot_general | solution.py:171
  337.7 42.4 %multiply_convert_fusion = (bf16[12,512,1024]{2,1,0:T(8,128)(2,1)}, bf16[12,512,1024]{2,1,0:T(8,128)(2,1)}) fusion(f32[12,512,1024]{2,1,0:T(8,128)} %get-tuple-element.81, f32[12,512]{1,0:T(8,128)S(1)} %get-tuple-element.80, f32[12,512]{1,0:T(8,128)S(1)} %log_add_fusion, f32[12,512,1024]{2,1,0:T(8,128)} %get-tuple-element.71, ...), kind=kLoop, calls=%fused_computation | loop fusion | flops 75497472 | bytes 126976000 | tf_op jit(solution)/shard_map/convert_element_type | solution.py:175
  380.0 10.7 %convolution_multiply_fusion = f32[12,64,512]{2,1,0:T(8,128)} fusion(bf16[1024,12,64]{0,2,1:T(8,128)(2,1)} %copy-done.3, bf16[12,512,1024]{2,1,0:T(8,128)(2,1)} %get-tuple-element.86), kind=kOutput, calls=%fused_computation.102 | convolution fusion | flops 805699584 | bytes 15728640 | tf_op jit(solution)/shard_map/hqk,khd->qhd/dot_general | solution.py:177
  390.7 6.6 convolution_multiply_fusion.1
  407.8 3.7 bitcast_multiply_fusion
  413.8 13.8 %fusion.4 = f32[12,64,1024]{2,1,0:T(8,128)} fusion(bf16[512,12,64]{0,2,1:T(8,128)(2,1)S(1)} %bitcast.92, f32[12,512]{1,0:T(8,128)S(1)} %log_add_fusion, f32[12,512,1024]{2,1,0:T(8,128)} %get-tuple-element.71, pred[512,1024]{1,0:T(8,128)(4,1)S(1)} %copy-done.18), kind=kOutput, calls=%fused_computation.16 | convolution fusion | flops 830472192 | bytes 29646848 | tf_op jit(solution)/shard_map/hqk,qhd->khd/dot_general | solution.py:168
  427.6 13.2 %add_convert_fusion.2 = bf16[12,64,1024]{2,1,0:T(8,128)(2,1)S(1)} fusion(f32[12,64,1024]{2,1,0:T(8,128)} %fusion.4, bf16[512,12,64]{0,2,1:T(8,128)(2,1)S(1)} %bitcast.90, f32[12,512]{1,0:T(8,128)S(1)} %log_add_fusion.1, f32[12,512,1024]{2,1,0:T(8,128)} %get-tuple-element.73, pred[512,1024]{1,0:T(8,128)(4,1)S(1)} %copy-done.15), kind=kOutput, calls=%fused_computation.80 | convolution fusion | flops 832045056 | bytes 31219712 | tf_op jit(solution)/shard_map/hqk,qhd->khd/dot_general | solution.py:168
  440.8 6.9 fusion.43
  447.7 5.5 add_convert_fusion.3
  455.0 7.0 fusion.30
  464.9 38.9 %all-reduce.5 = (f32[768]{0:T(1024)S(1)}, f32[768]{0:T(1024)S(1)}) all-reduce(f32[768]{0:T(1024)S(1)} %get-tuple-element.34, f32[768]{0:T(1024)S(1)} %copy-done.57), channel_id=6, replica_groups=mesh['fsdp'=32] {'fsdp'}, use_global_device_ids=true, to_apply=%region_21.22.clone | all-reduce | flops 1536 | bytes 12288
  505.0 5.5 add_convert_fusion.1
  516.4 124.4 %reduce-scatter.9.cloned.1.call-done = f32[72,768]{1,0:T(8,128)} async-done(((f32[2304,768]{1,0:T(8,128)}), f32[72,768]{1,0:T(8,128)}) %reduce-scatter.9.cloned.1.call-update) | async-done | bytes 221200 | tf_op jit(solution)/shard_map/reduce_scatter | solution.py:206
  640.8 125.4 %reduce-scatter.5.cloned.1.call-done = f32[72,768]{1,0:T(8,128)} async-done(((f32[2304,768]{1,0:T(8,128)}), f32[72,768]{1,0:T(8,128)}) %reduce-scatter.5.cloned.1.call-update) | async-done | bytes 221200 | tf_op jit(solution)/shard_map/reduce_scatter | solution.py:204
  (227 shorter events, 82.9 us)
Async XLA Ops:
  7.2 66.8 %all-gather.5.cloned.1.call-start = ((), (), s32[]{:S(2)}) async-start(), calls=%async_computation.3 | async-start | bytes 3649536 | tf_op jit(solution)/shard_map/all_gather | solution.py:80
  7.9 159.9 %all-gather.7.cloned.1.call-start = ((), (), s32[]{:S(2)}) async-start(), calls=%async_computation.4 | async-start | bytes 1216512 | tf_op jit(solution)/shard_map/all_gather | solution.py:81
  8.6 183.1 %all-gather.9.cloned.1.call-start = ((), (), s32[]{:S(2)}) async-start(), calls=%async_computation.5 | async-start | bytes 3649536 | tf_op jit(solution)/shard_map/all_gather | solution.py:82
  9.4 239.5 %all-gather.11.cloned.1.call-start = ((), (), s32[]{:S(2)}) async-start(), calls=%async_computation.6 | async-start | bytes 1824768 | tf_op jit(solution)/shard_map/all_gather | solution.py:83
  10.0 503.1 %all-reduce.9.cloned.1.call-start = ((), (), s32[]{:S(2)}) async-start(), calls=%async_computation.10 | async-start | bytes 7077888
  56.2 17.8 %copy-start.47 = (f32[768]{0:T(1024)}, f32[768]{0:T(1024)S(1)}, u32[]{:S(2)}) copy-start(f32[768]{0:T(1024)S(1)} %convert_element_type.75) | copy-start | bytes 9220
  59.3 37.4 %copy-start.27 = (f32[1024,64]{0,1:T(8,128)}, f32[1024,64]{0,1:T(8,128)S(1)}, u32[]{:S(2)}) copy-start(f32[1024,64]{0,1:T(8,128)S(1)} %get-tuple-element.63) | copy-start | bytes 786436
  61.2 106.6 %copy-start.1 = (bf16[1024,768]{0,1:T(8,128)(2,1)}, bf16[1024,768]{0,1:T(8,128)(2,1)S(1)}, u32[]{:S(2)}) copy-start(bf16[1024,768]{0,1:T(8,128)(2,1)S(1)} %copy.42) | copy-start | bytes 4718596
  61.5 18.7 %copy-start.45 = (f32[1024]{0:T(1024)}, f32[1024]{0:T(1024)S(1)}, u32[]{:S(2)}) copy-start(f32[1024]{0:T(1024)S(1)} %broadcast_multiply_fusion.4) | copy-start | bytes 12292
  62.6 17.6 %copy-start.49 = (f32[1024]{0:T(1024)}, f32[1024]{0:T(1024)S(1)}, u32[]{:S(2)}) copy-start(f32[1024]{0:T(1024)S(1)} %fusion.65) | copy-start | bytes 12292
  110.9 22.6 %copy-start.40 = (f32[12,512]{1,0:T(8,128)}, f32[12,512]{1,0:T(8,128)S(1)}, u32[]{:S(2)}) copy-start(f32[12,512]{1,0:T(8,128)S(1)} %get-tuple-element.70) | copy-start | bytes 73732
  133.5 13.9 %copy-start.42 = (f32[12,512]{1,0:T(8,128)}, f32[12,512]{1,0:T(8,128)S(1)}, u32[]{:S(2)}) copy-start(f32[12,512]{1,0:T(8,128)S(1)} %fusion.1) | copy-start | bytes 73732
  133.5 13.9 %slice-start = ((s8[25165824]{0:T(1024)(128)(4,1)}), s8[4194304]{0:T(1024)(128)(4,1)S(1)}, s32[]{:S(2)}) async-start(s8[25165824]{0:T(1024)(128)(4,1)} %bitcast.73), calls=%async_computation.11 | async-start | bytes 8388608
  133.5 13.9 %slice-start.1 = ((s8[25165824]{0:T(1024)(128)(4,1)}), s8[4194304]{0:T(1024)(128)(4,1)S(1)}, s32[]{:S(2)}) async-start(s8[25165824]{0:T(1024)(128)(4,1)} %bitcast.73), calls=%async_computation.12 | async-start | bytes 8388608
  133.5 13.9 %slice-start.2 = ((s8[25165824]{0:T(1024)(128)(4,1)}), s8[4194304]{0:T(1024)(128)(4,1)S(1)}, s32[]{:S(2)}) async-start(s8[25165824]{0:T(1024)(128)(4,1)} %bitcast.73), calls=%async_computation.13 | async-start | bytes 8388608
  133.5 13.9 %slice-start.3 = ((s8[25165824]{0:T(1024)(128)(4,1)}), s8[4194304]{0:T(1024)(128)(4,1)S(1)}, s32[]{:S(2)}) async-start(s8[25165824]{0:T(1024)(128)(4,1)} %bitcast.73), calls=%async_computation.14 | async-start | bytes 8388608
  133.5 14.6 %slice-start.4 = ((s8[25165824]{0:T(1024)(128)(4,1)}), s8[4194304]{0:T(1024)(128)(4,1)S(1)}, s32[]{:S(2)}) async-start(s8[25165824]{0:T(1024)(128)(4,1)} %bitcast.73), calls=%async_computation.15 | async-start | bytes 8388608
  133.6 15.8 %slice-start.5 = ((s8[25165824]{0:T(1024)(128)(4,1)}), s8[4194304]{0:T(1024)(128)(4,1)S(1)}, s32[]{:S(2)}) async-start(s8[25165824]{0:T(1024)(128)(4,1)} %bitcast.73), calls=%async_computation.16 | async-start | bytes 8388608
  171.0 20.8 %copy-start.55 = (f32[768]{0:T(1024)S(1)}, f32[768]{0:T(1024)}, u32[]{:S(2)}) copy-start(f32[768]{0:T(1024)} %convert_element_type.84) | copy-start | bytes 9220
  173.0 75.9 %copy-start.34 = (bf16[1024,768]{1,0:T(8,128)(2,1)S(1)}, bf16[1024,768]{1,0:T(8,128)(2,1)}, u32[]{:S(2)}) copy-start(bf16[1024,768]{1,0:T(8,128)(2,1)} %param.17) | copy-start | bytes 4718596
  248.9 16.1 %copy-start.23 = (f32[1024,2304]{1,0:T(8,128)S(1)}, f32[1024,2304]{1,0:T(8,128)}, u32[]{:S(2)}) copy-start(f32[1024,2304]{1,0:T(8,128)} %fusion.79) | copy-start | bytes 28311556
  273.1 243.2 %reduce-scatter.7.cloned.1.call-start = ((), (), s32[]{:S(2)}) async-start(), calls=%async_computation.8 | async-start | bytes 2433024 | tf_op jit(solution)/shard_map/reduce_scatter | solution.py:205
  289.2 351.6 %reduce-scatter.9.cloned.1.call-start = ((), (), s32[]{:S(2)}) async-start(), calls=%async_computation.9 | async-start | bytes 7299072 | tf_op jit(solution)/shard_map/reduce_scatter | solution.py:206
  300.9 465.3 %reduce-scatter.5.cloned.1.call-start = ((), (), s32[]{:S(2)}) async-start(), calls=%async_computation.7 | async-start | bytes 7299072 | tf_op jit(solution)/shard_map/reduce_scatter | solution.py:204
  302.0 17.9 %copy-start.17 = (pred[512,1024]{1,0:T(8,128)(4,1)S(1)}, pred[512,1024]{1,0:T(8,128)(4,1)}, u32[]{:S(2)}) copy-start(pred[512,1024]{1,0:T(8,128)(4,1)} %get-tuple-element.65) | copy-start | bytes 1572868
  413.8 27.0 %copy-start.37 = (bf16[1024,12,64]{0,2,1:T(8,128)(2,1)}, bf16[1024,12,64]{0,2,1:T(8,128)(2,1)S(1)}, u32[]{:S(2)}) copy-start(bf16[1024,12,64]{0,2,1:T(8,128)(2,1)S(1)} %fusion.37) | copy-start | bytes 4718596
  413.8 13.8 %copy-start.15 = (pred[512,1024]{1,0:T(8,128)(4,1)S(1)}, pred[512,1024]{1,0:T(8,128)(4,1)}, u32[]{:S(2)}) copy-start(pred[512,1024]{1,0:T(8,128)(4,1)} %get-tuple-element.64) | copy-start | bytes 1572868
  413.8 13.8 %copy-start.24 = (bf16[512,768]{0,1:T(8,128)(2,1)S(1)}, bf16[512,768]{0,1:T(8,128)(2,1)}, u32[]{:S(2)}) copy-start(bf16[512,768]{0,1:T(8,128)(2,1)} %get-tuple-element.56) | copy-start | bytes 2359300
  427.6 13.2 %copy-start.36 = (bf16[1024,768]{0,1:T(8,128)(2,1)S(1)}, bf16[1024,768]{0,1:T(8,128)(2,1)}, u32[]{:S(2)}) copy-start(bf16[1024,768]{0,1:T(8,128)(2,1)} %fusion.36) | copy-start | bytes 4718596
  427.6 13.2 %copy-start.46 = (f32[1024]{0:T(1024)S(1)}, f32[1024]{0:T(1024)}, u32[]{:S(2)}) copy-start(f32[1024]{0:T(1024)} %copy-done.45) | copy-start | bytes 12292
  462.0 43.0 %copy-start.10 = (bf16[1024,768]{0,1:T(8,128)(2,1)S(1)}, bf16[1024,768]{0,1:T(8,128)(2,1)}, u32[]{:S(2)}) copy-start(bf16[1024,768]{0,1:T(8,128)(2,1)} %copy.47) | copy-start | bytes 4718596
  462.0 43.0 %copy-start.54 = (f32[1024]{0:T(1024)S(1)}, f32[1024]{0:T(1024)}, u32[]{:S(2)}) copy-start(f32[1024]{0:T(1024)} %copy-done.53) | copy-start | bytes 12292
  (46 other events, 202.0 us)
Sparse Core Ops, SparseCore 0:
  10.9 63.0 all-gather.4
  76.9 52.8 all-gather.6
  132.7 58.9 all-gather.8
  194.5 54.4 all-gather.10
  273.2 137.8 all-reduce.8
  417.7 98.5 reduce-scatter.6
  522.6 118.1 reduce-scatter.8
  648.0 118.1 reduce-scatter.4
where the time goes:
time: 783 us; the launch traced here: 773 us
  waiting for transfers between devices  326 us (42%)
  matrix products  212 us (27%)
  other arithmetic  93.8 us (12%)
  blocking collectives  81.1 us (10%)
  local copies, waits for them, and re-layouts  44.4 us (6%)
  between operations  15.2 us (2%)
    reduce_scatter x1, waiting for transfers between devices, local(): lax.psum_scatter(grad_project_in, 'fsdp', scatter_dimension=0, tiled=True)  125 us
    reduce_scatter x1, waiting for transfers between devices, local(): lax.psum_scatter(grad_expand, 'fsdp', scatter_dimension=0, tiled=True)  124 us
    unnamed x2, blocking collectives  81.1 us
    all_gather x1, waiting for transfers between devices, local(): lax.all_gather(shrink_weight, 'fsdp', axis=0, tiled=True)  46.4 us
    convert_element_type x1, other arithmetic, local(): grad_scores = (probs * (grad_probs - row_dot)).astype(jnp.bfloat16)  42.4 us
    dot_general x2, matrix products, local(): jnp.einsum('qhd,khd->hqk', grad_block, values_low, preferred_element_type...  35.7 us
    unnamed x150, local copies, waits for them, and re-layouts  29 us
    dot_general x2, matrix products, local(): jnp.einsum('hqk,qhd->khd', probs_low, grad_block, preferred_element_type=...  26.9 us
  transfers between devices with their start and end apart: 8, of which 6 were waited for; matrix products, arithmetic and copies ran while one was open for 40% of the time, Pallas kernels for 0%

commit v1 on v0

v1 whole, which is shorter than its diff:
```python
import functools

import jax
import jax.numpy as jnp
from jax import lax
from jax.experimental import pallas as pl
from jax.experimental.pallas import tpu as pltpu
from jax.sharding import PartitionSpec as P

D = 768
HEADS = 12
HEAD_DIM = 64
FF = 1152


eps_norm = 1e-05
rope_base = 160000.0
masked_score = -1e30


def layer_norm(values, gain):
    center = jnp.mean(values, axis=-1, keepdims=True)
    centred = values - center
    spread = jnp.mean(centred * centred, axis=-1, keepdims=True)
    return centred * lax.rsqrt(spread + eps_norm) * gain


def gated_gelu(gate, upward):
    return jax.nn.gelu(gate, approximate=False) * upward


BQ = 256
PAIR = 2 * HEAD_DIM
STEP = 128


def swap_halves(values):
    lane = lax.broadcasted_iota(jnp.int32, values.shape, 1)
    low_half = lane % HEAD_DIM < HEAD_DIM // 2
    up = pltpu.roll(values, PAIR - HEAD_DIM // 2, 1)
    down = pltpu.roll(values, HEAD_DIM // 2, 1)
    return jnp.where(low_half, up, down)


def dot_nt(left, right):
    return lax.dot_general(
        left, right, (((1,), (1,)), ((), ())), preferred_element_type=jnp.float32
    )


def dot_nn(left, right):
    return jnp.dot(left, right, preferred_element_type=jnp.float32)


def attend_kernel(
    lo_ref, width_ref, q_ref, k_ref, v_ref, cos_ref, sin_ref, code_row_ref, code_col_ref,
    qr_ref, kr_ref, vr_ref, mixed_ref, lse_ref, vt_ref,
):
    number = pl.program_id(1)
    total = k_ref.shape[0]

    @pl.when(number == 0)
    def _():
        keys = k_ref[...]
        kr_ref[...] = (keys * cos_ref[...] + swap_halves(keys) * sin_ref[...]).astype(jnp.bfloat16)
        vr_ref[...] = v_ref[...].astype(jnp.bfloat16)
        vt_ref[...] = v_ref[...].T.astype(jnp.bfloat16)

    rows = pl.ds(pl.multiple_of(number * BQ, BQ), BQ)
    queries = q_ref[...]
    queries = queries * cos_ref[rows, :] + swap_halves(queries) * sin_ref[rows, :]
    queries = queries.astype(jnp.bfloat16) * jnp.bfloat16(HEAD_DIM**-0.5)
    qr_ref[...] = queries
    start = pl.multiple_of(lo_ref[number] * STEP, STEP)

    for quarter in range(1, total // BQ + 1):
        width = quarter * BQ

        @pl.when(width_ref[number] == quarter)
        def _():
            window = pl.ds(start, width)
            allowed = code_col_ref[window, :1] == code_row_ref[:1, :]
            outs = []
            for side in range(2):
                part = slice(side * HEAD_DIM, (side + 1) * HEAD_DIM)
                scores = dot_nt(kr_ref[window, part], queries[:, part])
                scores = jnp.where(allowed, scores, masked_score)
                peak = jnp.max(scores, axis=0, keepdims=True)
                shifted = jnp.exp(scores - peak)
                amount = jnp.sum(shifted, axis=0, keepdims=True)
                lse_ref[0, side : side + 1, :] = peak + jnp.log(amount)
                out = dot_nn(vt_ref[part, window], shifted.astype(jnp.bfloat16))
                outs.append(out * (1.0 / amount))
            mixed_ref[...] = jnp.concatenate(outs, axis=0).T.astype(jnp.bfloat16)


def attend_back_kernel(
    lo_ref, width_ref, qr_ref, kr_ref, vr_ref, gm_ref, lse_ref, cos_ref, sin_ref,
    code_row_ref, code_col_ref, gq_ref, gk_ref, gv_ref, kt_ref, gk_sum, gv_sum,
):
    number = pl.program_id(1)
    total = kr_ref.shape[0]

    @pl.when(number == 0)
    def _():
        kt_ref[...] = kr_ref[...].astype(jnp.float32).T.astype(jnp.bfloat16)
        gk_sum[...] = jnp.zeros_like(gk_sum)
        gv_sum[...] = jnp.zeros_like(gv_sum)

    rows = pl.ds(pl.multiple_of(number * BQ, BQ), BQ)
    queries = qr_ref[...]
    grads = gm_ref[...]
    start = pl.multiple_of(lo_ref[number] * STEP, STEP)

    for quarter in range(1, total // BQ + 1):
        width = quarter * BQ

        @pl.when(width_ref[number] == quarter)
        def _():
            window = pl.ds(start, width)
            allowed = code_col_ref[window, :1] == code_row_ref[:1, :]
            outs, key_parts, value_parts = [], [], []
            for side in range(2):
                part = slice(side * HEAD_DIM, (side + 1) * HEAD_DIM)
                scores = dot_nt(kr_ref[window, part], queries[:, part])
                scores = jnp.where(allowed, scores, masked_score)
                probs = jnp.exp(scores - lse_ref[0, side : side + 1, :])
                value_parts.append(dot_nn(probs.astype(jnp.bfloat16), grads[:, part]))
                weighted = probs * dot_nt(vr_ref[window, part], grads[:, part])
                row_dot = jnp.sum(weighted, axis=0, keepdims=True)
                grad_scores = (weighted - probs * row_dot).astype(jnp.bfloat16)
                key_parts.append(dot_nn(grad_scores, queries[:, part]))
                outs.append(dot_nn(kt_ref[part, window], grad_scores))
            gv_sum[window, :] += jnp.concatenate(value_parts, axis=1)
            gk_sum[window, :] += jnp.concatenate(key_parts, axis=1)
            out = jnp.concatenate(outs, axis=0).T * HEAD_DIM**-0.5
            gq_ref[...] = (
                out * cos_ref[rows, :] - swap_halves(out) * sin_ref[rows, :]
            ).astype(jnp.bfloat16)

    @pl.when(number == pl.num_programs(1) - 1)
    def _():
        keys = gk_sum[...]
        gk_ref[...] = (keys * cos_ref[...] - swap_halves(keys) * sin_ref[...]).astype(jnp.bfloat16)
        gv_ref[...] = gv_sum[...].astype(jnp.bfloat16)


def attention_tables(segment_ids):
    slot_count = segment_ids.shape[0]
    slots = jnp.arange(slot_count, dtype=jnp.int32)
    same = segment_ids[:, None] == segment_ids[None, :]
    starts = jnp.min(jnp.where(same, slots[None, :], slot_count), axis=1)
    ends = jnp.max(jnp.where(same, slots[None, :], -1), axis=1) + 1
    padding = segment_ids < 0
    code = jnp.where(padding, -1 - slots, segment_ids)
    first = jnp.where(padding, slots, starts)[::BQ] // STEP
    last = (jnp.where(padding, slots + 1, ends)[BQ - 1 :: BQ] + STEP - 1) // STEP
    ratio = BQ // STEP
    width = (last - first + ratio - 1) // ratio
    lo = jnp.minimum(first, slot_count // STEP - ratio * width)
    position = (slots - starts).astype(jnp.float32)
    lane = jnp.arange(PAIR, dtype=jnp.int32)
    half = HEAD_DIM // 2
    freq = rope_base ** (-(lane % half).astype(jnp.float32) * 2.0 / HEAD_DIM)
    angle = position[:, None] * freq[None, :]
    sign = jnp.where(lane % HEAD_DIM < half, -1.0, 1.0)
    code_row = jnp.broadcast_to(code[None, :], (8, slot_count))
    code_col = jnp.broadcast_to(code[:, None], (slot_count, STEP))
    return lo, width, jnp.cos(angle), jnp.sin(angle) * sign[None, :], code_row, code_col


def table_specs(slot_count):
    return (
        [pl.BlockSpec((slot_count, PAIR), lambda h, i, *_: (0, 0))] * 2,
        [
            pl.BlockSpec((8, BQ), lambda h, i, *_: (0, i)),
            pl.BlockSpec((slot_count, STEP), lambda h, i, *_: (0, 0)),
        ],
    )


def attend(joined, tables):
    lo, width, cosine, sine, code_row, code_col = tables
    slot_count = joined.shape[0]
    pairs = D // PAIR
    rope_specs, code_specs = table_specs(slot_count)
    block = pl.BlockSpec((BQ, PAIR), lambda h, i, *_: (i, h))
    whole = lambda shift: pl.BlockSpec((slot_count, PAIR), lambda h, i, *_: (0, h + shift))
    wide = jax.ShapeDtypeStruct((slot_count, D), jnp.bfloat16)
    return pl.pallas_call(
        attend_kernel,
        grid_spec=pltpu.PrefetchScalarGridSpec(
            num_scalar_prefetch=2,
            grid=(pairs, slot_count // BQ),
            in_specs=[block, whole(pairs), whole(2 * pairs)] + rope_specs + code_specs,
            out_specs=[
                block, whole(0), whole(0), block,
                pl.BlockSpec((1, 8, BQ), lambda h, i, *_: (h, 0, i)),
            ],
            scratch_shapes=[pltpu.VMEM((PAIR, slot_count), jnp.bfloat16)],
        ),
        out_shape=[wide, wide, wide, wide,
                   jax.ShapeDtypeStruct((pairs, 8, slot_count), jnp.float32)],
        compiler_params=pltpu.CompilerParams(vmem_limit_bytes=40 * 2**20),
        cost_estimate=pl.CostEstimate(
            flops=16 * slot_count * slot_count * D, bytes_accessed=24 * slot_count * D,
            transcendentals=HEADS * slot_count * slot_count),
    )(lo, width, joined, joined, joined, cosine, sine, code_row, code_col)


def attend_back(qr, kr, vr, grad_mixed, lse, tables):
    lo, width, cosine, sine, code_row, code_col = tables
    slot_count = qr.shape[0]
    pairs = D // PAIR
    rope_specs, code_specs = table_specs(slot_count)
    block = pl.BlockSpec((BQ, PAIR), lambda h, i, *_: (i, h))
    whole = pl.BlockSpec((slot_count, PAIR), lambda h, i, *_: (0, h))
    wide = jax.ShapeDtypeStruct((slot_count, D), jnp.bfloat16)
    return pl.pallas_call(
        attend_back_kernel,
        grid_spec=pltpu.PrefetchScalarGridSpec(
            num_scalar_prefetch=2,
            grid=(pairs, slot_count // BQ),
            in_specs=[block, whole, whole, block,
                      pl.BlockSpec((1, 8, BQ), lambda h, i, *_: (h, 0, i))]
            + rope_specs + code_specs,
            out_specs=[block, whole, whole],
            scratch_shapes=[
                pltpu.VMEM((PAIR, slot_count), jnp.bfloat16),
                pltpu.VMEM((slot_count, PAIR), jnp.float32),
                pltpu.VMEM((slot_count, PAIR), jnp.float32),
            ],
        ),
        out_shape=[wide, wide, wide],
        compiler_params=pltpu.CompilerParams(vmem_limit_bytes=40 * 2**20),
        cost_estimate=pl.CostEstimate(
            flops=40 * slot_count * slot_count * D, bytes_accessed=20 * slot_count * D,
            transcendentals=HEADS * slot_count * slot_count),
    )(lo, width, qr, kr, vr, grad_mixed, lse, cosine, sine, code_row, code_col)


def halving_sum(partial, order, device_count, kind):
    bits = device_count.bit_length() - 1
    me = lax.axis_index("fsdp")
    rows, cols = partial.shape[0] // device_count, partial.shape[1]
    current = partial.reshape((2,) * bits + (rows, cols))
    for bit in order:
        axis = bits - 1 - bit
        mine = (me >> bit) & 1
        keep = lax.dynamic_slice_in_dim(current, mine, 1, axis)
        send = lax.dynamic_slice_in_dim(current, 1 - mine, 1, axis).astype(kind)
        pairs = [(index, index ^ (1 << bit)) for index in range(device_count)]
        current = keep + lax.ppermute(send, "fsdp", pairs).astype(jnp.float32)
    return current.reshape(rows, cols)


def exchange_orders(device_count):
    bits = device_count.bit_length() - 1
    middle = list(range(1, bits - 1))
    turns = [middle[t:] + middle[:t] for t in range(min(3, len(middle)))] or [middle]
    ends = [bits - 1] if bits > 1 else []
    return [[0] + turn + ends for turn in turns]


def summed_to_owners(partial, device_count):
    orders = exchange_orders(device_count)
    cols = partial.shape[1] // len(orders)
    return jnp.concatenate(
        [
            halving_sum(partial[:, t * cols : (t + 1) * cols], order, device_count, jnp.bfloat16)
            for t, order in enumerate(orders)
        ],
        axis=1,
    )


def doubling_gather(block, device_count):
    me = lax.axis_index("fsdp")
    current = block
    for bit in range(device_count.bit_length() - 1):
        pairs = [(index, index ^ (1 << bit)) for index in range(device_count)]
        other = lax.ppermute(current, "fsdp", pairs)
        upper = (me >> bit) & 1 == 1
        current = jnp.concatenate(
            [jnp.where(upper, other, current), jnp.where(upper, current, other)], axis=0
        )
    return current


def gains_to_owners(gain_one, gain_two, device_count):
    own = gain_one.shape[0] // device_count
    both = jnp.stack([gain_one.reshape(device_count, own), gain_two.reshape(device_count, own)], 1)
    both = jnp.pad(both, ((0, 0), (0, 0), (0, 128 - own))).reshape(2 * device_count, 128)
    done = halving_sum(both, exchange_orders(device_count)[0], device_count, jnp.float32)
    return done[0, :own], done[1, :own]


def right_product(left, weight):
    return lax.dot_general(
        left, weight, (((1,), (1,)), ((), ())), preferred_element_type=jnp.float32
    )


def outer_sum(grads, inputs):
    return lax.dot_general(
        grads, inputs, (((0,), (0,)), ((), ())), preferred_element_type=jnp.float32
    )


def local(
    device_count,
    hidden_in,
    segment_ids,
    project_in,
    project_out,
    expand_weight,
    shrink_weight,
    first_gain,
    second_gain,
    cotangent,
):
    slot_count = hidden_in.shape[0]
    own_gain = first_gain.shape[0]
    both_gains = jnp.pad(jnp.stack([first_gain, second_gain]), ((0, 0), (0, 128 - own_gain)))
    gains = doubling_gather(both_gains[None], device_count)
    gain_one = gains[:, 0, :own_gain].reshape(device_count * own_gain)
    gain_two = gains[:, 1, :own_gain].reshape(device_count * own_gain)
    full_in = lax.all_gather(project_in, "fsdp", axis=0, tiled=True)
    full_out = lax.all_gather(project_out, "fsdp", axis=0, tiled=True)
    full_expand = lax.all_gather(expand_weight, "fsdp", axis=0, tiled=True)
    full_shrink = lax.all_gather(shrink_weight, "fsdp", axis=0, tiled=True)
    tables = attention_tables(segment_ids)
    hidden = hidden_in.astype(jnp.float32)
    normed, norm_back_one = jax.vjp(layer_norm, hidden, gain_one.astype(jnp.float32))
    normed_low = normed.astype(jnp.bfloat16)
    joined = right_product(normed_low, full_in)
    queries_low, keys_low, values_low, mixed_low, lse = attend(joined, tables)
    middle = hidden + right_product(mixed_low, full_out)
    normed_two, norm_back_two = jax.vjp(layer_norm, middle, gain_two.astype(jnp.float32))
    normed_two_low = normed_two.astype(jnp.bfloat16)
    widened = right_product(normed_two_low, full_expand)
    product, glu_back = jax.vjp(gated_gelu, widened[:, :FF], widened[:, FF:])
    product_low = product.astype(jnp.bfloat16)
    hidden_out = (middle + right_product(product_low, full_shrink)).astype(jnp.bfloat16)
    grad_shrink = outer_sum(cotangent, product_low)
    grad_product = jnp.dot(cotangent, full_shrink, preferred_element_type=jnp.float32)
    grad_gate, grad_upward = glu_back(grad_product)
    grad_wide = jnp.concatenate([grad_gate, grad_upward], axis=1).astype(jnp.bfloat16)
    grad_expand = outer_sum(grad_wide, normed_two_low)
    grad_normed_two = jnp.dot(grad_wide, full_expand, preferred_element_type=jnp.float32)
    grad_mid_norm, grad_gain_two = norm_back_two(grad_normed_two)
    grad_middle = cotangent.astype(jnp.float32) + grad_mid_norm
    grad_mid_low = grad_middle.astype(jnp.bfloat16)
    grad_project_out = outer_sum(grad_mid_low, mixed_low)
    grad_mixed = jnp.dot(grad_mid_low, full_out, preferred_element_type=jnp.float32).astype(
        jnp.bfloat16
    )
    owned_shrink = summed_to_owners(grad_shrink, device_count)
    owned_expand = summed_to_owners(grad_expand, device_count)
    owned_out = summed_to_owners(grad_project_out, device_count)
    grad_joined = jnp.concatenate(
        attend_back(queries_low, keys_low, values_low, grad_mixed, lse, tables), axis=1
    )
    grad_project_in = outer_sum(grad_joined, normed_low)
    grad_normed = jnp.dot(grad_joined, full_in, preferred_element_type=jnp.float32)
    grad_hidden_norm, grad_gain_one = norm_back_one(grad_normed)
    grad_input = (grad_middle + grad_hidden_norm).astype(jnp.bfloat16)
    owned_in = summed_to_owners(grad_project_in, device_count)
    owned_gain_one, owned_gain_two = gains_to_owners(grad_gain_one, grad_gain_two, device_count)
    return (
        hidden_out,
        grad_input,
        owned_in,
        owned_out,
        owned_expand,
        owned_shrink,
        owned_gain_one,
        owned_gain_two,
    )


def solution(mesh):
    return jax.shard_map(
        functools.partial(local, mesh.shape["fsdp"]),
        mesh=mesh,
        in_specs=(
            P("fsdp", None),
            P("fsdp"),
            P("fsdp", None),
            P("fsdp", None),
            P("fsdp", None),
            P("fsdp", None),
            P("fsdp"),
            P("fsdp"),
            P("fsdp", None),
        ),
        out_specs=(
            P("fsdp", None),
            P("fsdp", None),
            P("fsdp", None),
            P("fsdp", None),
            P("fsdp", None),
            P("fsdp", None),
            P("fsdp"),
            P("fsdp"),
        ),
        check_vma=False,
    )
```

time: 783 us -> 582 us (0.74)
  matrix products: 212 us -> 81.7 us
  Pallas kernels: 0 us -> 86.6 us
  blocking collectives: 81.1 us -> 0 us
  other arithmetic: 93.8 us -> 26.6 us
  waiting for transfers between devices: 326 us -> 268 us
  starting transfers between devices: 0.31 us -> 55.2 us
    reduce_scatter x3 -> x0, waiting for transfers between devices: 251 us -> none  [the longest x1 125 us: local(): lax.psum_scatter(grad_project_in, 'fsdp', scatter_dimension=0, tiled=True)]
    dot_general x16 -> x4, matrix products: 166 us -> 28.5 us  [the longest x1 16.1 us: local(): jnp.dot(cotangent, full_shrink, preferred_element_type=jnp.float32)]
    ppermute x0 -> x70, waiting for transfers between devices: none -> 121 us  [the longest x65 117 us: halving_sum(): current = keep + lax.ppermute(send, 'fsdp', pairs).astype(jnp.float32)]
    pallas_call x0 -> x2, Pallas kernels: none -> 86.6 us  [the longest x1 47.6 us: attend_back(): pl.pallas_call(attend_back_kernel, grid_spec=pltpu.PrefetchScalarGridSpec...]
    unnamed x2 -> x0, blocking collectives: 81.1 us -> none
    all_gather x4, waiting for transfers between devices: 72.8 us -> 145 us  [the longest x1 54.8 us: local(): full_expand = lax.all_gather(expand_weight, 'fsdp', axis=0, tiled=True)]
    ppermute x0 -> x70, starting transfers between devices: none -> 55.1 us  [the longest x65 44.6 us: halving_sum(): current = keep + lax.ppermute(send, 'fsdp', pairs).astype(jnp.float32)]
    convert_element_type x4 -> x0, other arithmetic: 44.3 us -> none  [the longest x1 42.4 us: local(): grad_scores = (probs * (grad_probs - row_dot)).astype(jnp.bfloat16)]
  transfers between devices with their start and end apart: 8 -> 74, of which waited for: 6 -> 44; matrix products, arithmetic and copies ran while one was open for 40% -> 13% of each run, Pallas kernels for 0% -> 7%
where the time goes in v1:
time: 582 us; the launch traced here: 571 us
  waiting for transfers between devices  268 us (46%)
  Pallas kernels  86.6 us (15%)
  matrix products  81.7 us (14%)
  starting transfers between devices  55.2 us (9%)
  local copies, waits for them, and re-layouts  36.8 us (6%)
  other arithmetic  26.6 us (5%)
  between operations  16 us (3%)
    ppermute x65, waiting for transfers between devices, halving_sum(): current = keep + lax.ppermute(send, 'fsdp', pairs).astype(jnp.float32)  117 us
    all_gather x1, waiting for transfers between devices, local(): full_expand = lax.all_gather(expand_weight, 'fsdp', axis=0, tiled=True)  54.8 us
    pallas_call x1, Pallas kernels, attend_back(): pl.pallas_call(attend_back_kernel, grid_spec=pltpu.PrefetchScalarGridSpec...  47.6 us
    all_gather x1, waiting for transfers between devices, local(): full_shrink = lax.all_gather(shrink_weight, 'fsdp', axis=0, tiled=True)  46.3 us
    ppermute x65, starting transfers between devices, halving_sum(): current = keep + lax.ppermute(send, 'fsdp', pairs).astype(jnp.float32)  44.6 us
    all_gather x1, waiting for transfers between devices, local(): full_in = lax.all_gather(project_in, 'fsdp', axis=0, tiled=True)  39.8 us
    pallas_call x1, Pallas kernels, attend(): pl.pallas_call(attend_kernel, grid_spec=pltpu.PrefetchScalarGridSpec(num_...  39 us
    dot_general x4, matrix products, right_product(): lax.dot_general(left, weight, (((1,), (1,)), ((), ())), preferred_element...  30 us
  transfers between devices with their start and end apart: 74, of which 44 were waited for; matrix products, arithmetic and copies ran while one was open for 13% of the time, Pallas kernels for 7%

profile of v1, /device:TPU:0, one launch (start us, length us, event | category | flops | bytes accessed | tf_op | source)
XLA Modules:
  0.0 571.0 jit_solution(11491004630603059116)
XLA Ops:
  33.9 39.8 %all-gather.5.cloned.1.call-done = bf16[2304,768]{1,0:T(8,128)(2,1)} async-done(((bf16[72,768]{1,0:T(8,128)(2,1)}), bf16[2304,768]{1,0:T(8,128)(2,1)}) %all-gather.5.cloned.1.call-update) | async-done | bytes 3538960 | tf_op jit(solution)/shard_map/all_gather | solution.py:328
  73.8 8.7 %fusion.26.q_ref.k_ref.v_ref = f32[1024,2304]{1,0:T(8,128)} fusion(bf16[2304,768]{1,0:T(8,128)(2,1)} %all-gather.5.cloned.1.call-done, bf16[1024,768]{0,1:T(8,128)(2,1)S(1)} %copy.29, f32[768]{0:T(1024)S(1)} %reshape.221, f32[1024]{0:T(1024)S(1)} %fusion.42, f32[1024]{0:T(1024)S(1)} %broadcast_multiply_fusion.1), kind=kOutput, calls=%fused_computation.111 | convolution fusion | flops 3627810816 | bytes 14560256 | tf_op jit(solution)/shard_map/dot_general | solution.py:299
  82.7 39.0 %shard_map.152 = (bf16[1024,768]{1,0:T(8,128)(2,1)S(1)}, bf16[1024,768]{1,0:T(8,128)(2,1)S(1)}, bf16[1024,768]{1,0:T(8,128)(2,1)S(1)}, bf16[1024,768]{1,0:T(8,128)(2,1)S(1)}, f32[6,8,1024]{2,1,0:T(8,128)S(1)}) custom-call(s32[4]{0:T(128)S(1)} %get-tuple-element.60.lo_ref, s32[4]{0:T(128)S(1)} %get-tuple-element.61.width_ref, ...), custom_call_target="tpu_custom_call" | custom-call | flops 12884901888 | bytes 18874368 | tf_op jit(solution)/shard_map/pallas_call | solution.py:190
  125.2 4.5 all-gather.7.cloned.1.call-done
  129.7 4.9 fusion.64
  136.9 54.8 %all-gather.9.cloned.1.call-done = bf16[2304,768]{1,0:T(8,128)(2,1)} async-done(((bf16[72,768]{1,0:T(8,128)(2,1)}), bf16[2304,768]{1,0:T(8,128)(2,1)}) %all-gather.9.cloned.1.call-update) | async-done | bytes 3538960 | tf_op jit(solution)/shard_map/all_gather | solution.py:330
  191.7 10.8 %fusion.57 = f32[1024,2304]{1,0:T(8,128)} fusion(bf16[2304,768]{1,0:T(8,128)(2,1)} %all-gather.9.cloned.1.call-done, f32[1024,768]{0,1:T(8,128)} %get-tuple-element.97, f32[768]{0:T(1024)S(1)} %reshape.222, f32[1024]{0:T(1024)S(1)} %fusion.43, f32[1024]{0:T(1024)S(1)} %broadcast_multiply_fusion), kind=kOutput, calls=%fused_computation.275 | convolution fusion | flops 3627024384 | bytes 16133120 | tf_op jit(solution)/shard_map/dot_general | solution.py:299
  202.5 46.3 %all-gather.11.cloned.1.call-done = bf16[768,1152]{1,0:T(8,128)(2,1)} async-done(((bf16[24,1152]{1,0:T(8,128)(2,1)}), bf16[768,1152]{1,0:T(8,128)(2,1)}) %all-gather.11.cloned.1.call-update) | async-done | bytes 1769488 | tf_op jit(solution)/shard_map/all_gather | solution.py:331
  248.8 16.1 %add_convert_fusion = (bf16[1024,1152]{1,0:T(8,128)(2,1)}, f32[1024,1152]{1,0:T(8,128)S(1)}, f32[1024,1152]{1,0:T(8,128)S(1)}) fusion(f32[1024,2304]{1,0:T(8,128)} %fusion.57, bf16[1024,768]{1,0:T(8,128)(2,1)} %param.17, bf16[768,1152]{1,0:T(8,128)(2,1)} %all-gather.11.cloned.1.call-done), kind=kOutput, calls=%fused_computation.15 | convolution fusion | flops 1898053632 | bytes 24576000 | tf_op jit(solution)/shard_map/dot_general | solution.py:346
  267.7 9.7 %fusion.19 = f32[2304,768]{1,0:T(8,128)} fusion(bf16[1024,1152]{1,0:T(8,128)(2,1)S(1)} %get-tuple-element.62, bf16[1024,1152]{1,0:T(8,128)(2,1)} %get-tuple-element.58, f32[1024,768]{0,1:T(8,128)} %get-tuple-element.97, f32[768]{0:T(1024)S(1)} %reshape.222, f32[1024]{0:T(1024)S(1)} %fusion.43, f32[1024]{0:T(1024)S(1)} %broadcast_multiply_fusion), kind=kOutput, calls=%fused_computation.48 | convolution fusion | flops 3636461568 | bytes 14953472 | tf_op jit(solution)/shard_map/dot_general | solution.py:305
  277.4 6.7 %multiply_reduce_fusion = (f32[768]{0:T(1024)S(1)}, f32[1024]{0:T(1024)S(1)}, f32[1024,768]{0,1:T(8,128)S(1)}) fusion(f32[1024,768]{0,1:T(8,128)} %get-tuple-element.97, f32[1024]{0:T(1024)S(1)} %fusion.43, f32[1024]{0:T(1024)S(1)} %broadcast_multiply_fusion, f32[768]{0:T(1024)S(1)} %reshape.222, bf16[2304,768]{1,0:T(8,128)(2,1)S(1)} %copy-done.57, ...), kind=kOutput, calls=%fused_computation.41 | convolution fusion | flops 3638819072 | bytes 14567424 | tf_op jit(solution)/shard_map/dot_general | solution.py:350
  293.9 47.6 %shard_map.153 = (bf16[1024,768]{1,0:T(8,128)(2,1)S(1)}, bf16[1024,768]{1,0:T(8,128)(2,1)S(1)}, bf16[1024,768]{1,0:T(8,128)(2,1)S(1)}) custom-call(s32[4]{0:T(128)S(1)} %get-tuple-element.60.lo_ref, s32[4]{0:T(128)S(1)} %get-tuple-element.61.width_ref, bf16[1024,768]{1,0:T(8,128)(2,1)S(1)} %copy-done.1, bf16[1024,768]{1,0:T(8,128)(2,1)S(1)} %copy-done.3, ...), custom_call_target="tpu_custom_call" | custom-call | flops 32212254720 | bytes 15728640 | tf_op jit(solution)/shard_map/pallas_call | solution.py:219
  343.0 6.4 %fusion.24 = f32[2304,768]{1,0:T(8,128)} fusion(bf16[1024,2304]{1,0:T(8,128)(2,1)S(1)} %constant_dynamic-update-slice_fusion, bf16[1024,768]{0,1:T(8,128)(2,1)S(1)} %copy-done.7, f32[768]{0:T(1024)S(1)} %copy-done.48, f32[1024]{0:T(1024)S(1)} %copy-done.50, f32[1024]{0:T(1024)S(1)} %copy-done.46), kind=kOutput, calls=%fused_computation.110 | convolution fusion | flops 3627810816 | bytes 13380608 | tf_op jit(solution)/shard_map/dot_general | solution.py:305
  349.4 4.1 fusion.18
  356.9 4.2 convolution_bitcast_fusion
  378.4 5.5 add_convert_fusion.2
  413.4 4.0 collective-permute-done.21
  417.7 4.3 collective-permute-done.26
  422.5 4.1 collective-permute-done.31
  450.4 4.7 collective-permute-done.24
  455.1 4.7 collective-permute-done.29
  459.8 4.6 collective-permute-done.34
  465.5 4.1 collective-permute-done.51
  470.0 4.7 collective-permute-done.56
  475.2 4.6 collective-permute-done.61
  480.3 3.9 collective-permute-done.52
  484.7 3.9 collective-permute-done.57
  489.0 3.9 collective-permute-done.62
  505.0 4.7 collective-permute-done.54
  509.7 4.8 collective-permute-done.59
  514.5 4.7 collective-permute-done.64
  527.7 4.1 collective-permute-done.36
  (454 shorter events, 175.9 us)
Async XLA Ops:
  7.2 66.6 %all-gather.5.cloned.1.call-start = ((), (), s32[]{:S(2)}) async-start(), calls=%async_computation | async-start | bytes 3649536 | tf_op jit(solution)/shard_map/all_gather | solution.py:328
  7.9 121.8 %all-gather.7.cloned.1.call-start = ((), (), s32[]{:S(2)}) async-start(), calls=%async_computation.1 | async-start | bytes 1216512 | tf_op jit(solution)/shard_map/all_gather | solution.py:329
  8.7 183.0 %all-gather.9.cloned.1.call-start = ((), (), s32[]{:S(2)}) async-start(), calls=%async_computation.2 | async-start | bytes 3649536 | tf_op jit(solution)/shard_map/all_gather | solution.py:330
  9.4 239.4 %all-gather.11.cloned.1.call-start = ((), (), s32[]{:S(2)}) async-start(), calls=%async_computation.3 | async-start | bytes 1824768 | tf_op jit(solution)/shard_map/all_gather | solution.py:331
  356.8 28.0 %collective-permute-start.65 = (f32[2,2,2,2,1,2,128]{6,5,4,3,2,1,0:T(2,128)S(1)}, f32[2,2,2,2,1,2,128]{6,5,4,3,2,1,0:T(2,128)S(1)}, u32[]{:S(2)}, u32[]{:S(2)}) collective-permute-start(f32[2,2,2,2,1,2,128]{6,5,4,3,2,1,0:T(2,128)S(1)} %copy.38), channel_id=1, source_target_pairs={{0,1},{1,0},{2,3},{3,2},{4,5},{5,4},{6,7},{7,6},{8,9},{9,8},{10,11... | collective-permute-start | bytes 49160 | tf_op jit(solution)/shard_map/ppermute | solution.py:253
  362.2 47.3 %collective-permute-start.50 = (bf16[2,2,2,2,1,24,384]{6,5,4,3,2,1,0:T(8,128)(2,1)}, bf16[2,2,2,2,1,24,384]{6,5,4,3,2,1,0:T(8,128)(2,1)}, u32[]{:S(2)}, u32[]{:S(2)}) collective-permute-start(bf16[2,2,2,2,1,24,384]{6,5,4,3,2,1,0:T(8,128)(2,1)} %dynamic-slice_convert_fusion.8), channel_id=1, source_target_pairs={{0,1},{1,0},{2,3},{3,2},{4,5},{5,4},{6,7},{7,6},{8,9},{9,8},{10,11... | collective-permute-start | bytes 884744 | tf_op jit(solution)/shard_map/ppermute | solution.py:253
  363.4 47.5 %collective-permute-start.55 = (bf16[2,2,2,2,1,24,384]{6,5,4,3,2,1,0:T(8,128)(2,1)}, bf16[2,2,2,2,1,24,384]{6,5,4,3,2,1,0:T(8,128)(2,1)}, u32[]{:S(2)}, u32[]{:S(2)}) collective-permute-start(bf16[2,2,2,2,1,24,384]{6,5,4,3,2,1,0:T(8,128)(2,1)} %dynamic-slice_convert_fusion.7), channel_id=1, source_target_pairs={{0,1},{1,0},{2,3},{3,2},{4,5},{5,4},{6,7},{7,6},{8,9},{9,8},{10,11... | collective-permute-start | bytes 884744 | tf_op jit(solution)/shard_map/ppermute | solution.py:253
  364.4 47.9 %collective-permute-start.60 = (bf16[2,2,2,2,1,24,384]{6,5,4,3,2,1,0:T(8,128)(2,1)}, bf16[2,2,2,2,1,24,384]{6,5,4,3,2,1,0:T(8,128)(2,1)}, u32[]{:S(2)}, u32[]{:S(2)}) collective-permute-start(bf16[2,2,2,2,1,24,384]{6,5,4,3,2,1,0:T(8,128)(2,1)} %dynamic-slice_convert_fusion.6), channel_id=1, source_target_pairs={{0,1},{1,0},{2,3},{3,2},{4,5},{5,4},{6,7},{7,6},{8,9},{9,8},{10,11... | collective-permute-start | bytes 884744 | tf_op jit(solution)/shard_map/ppermute | solution.py:253
  366.4 153.5 %collective-permute-start.35 = (bf16[2,2,2,2,1,72,256]{6,5,4,3,2,1,0:T(8,128)(2,1)}, bf16[2,2,2,2,1,72,256]{6,5,4,3,2,1,0:T(8,128)(2,1)}, u32[]{:S(2)}, u32[]{:S(2)}) collective-permute-start(bf16[2,2,2,2,1,72,256]{6,5,4,3,2,1,0:T(8,128)(2,1)} %dynamic-slice_convert_fusion.2), channel_id=1, source_target_pairs={{0,1},{1,0},{2,3},{3,2},{4,5},{5,4},{6,7},{7,6},{8,9},{9,8},{10,11... | collective-permute-start | bytes 1769480 | tf_op jit(solution)/shard_map/ppermute | solution.py:253
  395.8 8.6 %collective-permute-start.69 = (f32[1,1,1,1,1,2,128]{6,5,4,3,2,1,0:T(2,128)S(1)}, f32[1,1,1,1,1,2,128]{6,5,4,3,2,1,0:T(2,128)S(1)}, u32[]{:S(2)}, u32[]{:S(2)}) collective-permute-start(f32[1,1,1,1,1,2,128]{6,5,4,3,2,1,0:T(2,128)S(1)} %constant_dynamic-slice_fusion), channel_id=1, source_target_pairs={{0,16},{1,17},{2,18},{3,19},{4,20},{5,21},{6,22},{7,23},{8,24},{9,... | collective-permute-start | bytes 3080 | tf_op jit(solution)/shard_map/ppermute | solution.py:253
  409.2 112.6 %collective-permute-start.40 = (bf16[2,2,2,2,1,72,256]{6,5,4,3,2,1,0:T(8,128)(2,1)}, bf16[2,2,2,2,1,72,256]{6,5,4,3,2,1,0:T(8,128)(2,1)S(1)}, u32[]{:S(2)}, u32[]{:S(2)}) collective-permute-start(bf16[2,2,2,2,1,72,256]{6,5,4,3,2,1,0:T(8,128)(2,1)} %dynamic-slice_convert_fusion.1), channel_id=1, source_target_pairs={{0,1},{1,0},{2,3},{3,2},{4,5},{5,4},{6,7},{7,6},{8,9},{9,8},{10,11... | collective-permute-start | bytes 1769480 | tf_op jit(solution)/shard_map/ppermute | solution.py:253
  409.5 112.7 %collective-permute-start.45 = (bf16[2,2,2,2,1,72,256]{6,5,4,3,2,1,0:T(8,128)(2,1)S(1)}, bf16[2,2,2,2,1,72,256]{6,5,4,3,2,1,0:T(8,128)(2,1)S(1)}, u32[]{:S(2)}, u32[]{:S(2)}) collective-permute-start(bf16[2,2,2,2,1,72,256]{6,5,4,3,2,1,0:T(8,128)(2,1)S(1)} %copy-done.42), channel_id=1, source_target_pairs={{0,1},{1,0},{2,3},{3,2},{4,5},{5,4},{6,7},{7,6},{8,9},{9,8},{10,11... | collective-permute-start | bytes 1769480 | tf_op jit(solution)/shard_map/ppermute | solution.py:253
  411.0 113.1 %collective-permute-start.5 = (bf16[2,2,2,2,1,72,256]{6,5,4,3,2,1,0:T(8,128)(2,1)S(1)}, bf16[2,2,2,2,1,72,256]{6,5,4,3,2,1,0:T(8,128)(2,1)S(1)}, u32[]{:S(2)}, u32[]{:S(2)}) collective-permute-start(bf16[2,2,2,2,1,72,256]{6,5,4,3,2,1,0:T(8,128)(2,1)S(1)} %copy-done.41), channel_id=1, source_target_pairs={{0,1},{1,0},{2,3},{3,2},{4,5},{5,4},{6,7},{7,6},{8,9},{9,8},{10,11... | collective-permute-start | bytes 1769480 | tf_op jit(solution)/shard_map/ppermute | solution.py:253
  519.2 6.9 %collective-permute-start.10 = (bf16[2,2,2,2,1,72,256]{6,5,4,3,2,1,0:T(8,128)(2,1)S(1)}, bf16[2,2,2,2,1,72,256]{6,5,4,3,2,1,0:T(8,128)(2,1)S(1)}, u32[]{:S(2)}, u32[]{:S(2)}) collective-permute-start(bf16[2,2,2,2,1,72,256]{6,5,4,3,2,1,0:T(8,128)(2,1)S(1)} %copy-done.43), channel_id=1, source_target_pairs={{0,1},{1,0},{2,3},{3,2},{4,5},{5,4},{6,7},{7,6},{8,9},{9,8},{10,11... | collective-permute-start | bytes 1769480 | tf_op jit(solution)/shard_map/ppermute | solution.py:253
  519.8 7.1 %collective-permute-start.15 = (bf16[2,2,2,2,1,72,256]{6,5,4,3,2,1,0:T(8,128)(2,1)S(1)}, bf16[2,2,2,2,1,72,256]{6,5,4,3,2,1,0:T(8,128)(2,1)S(1)}, u32[]{:S(2)}, u32[]{:S(2)}) collective-permute-start(bf16[2,2,2,2,1,72,256]{6,5,4,3,2,1,0:T(8,128)(2,1)S(1)} %copy-done.44), channel_id=1, source_target_pairs={{0,1},{1,0},{2,3},{3,2},{4,5},{5,4},{6,7},{7,6},{8,9},{9,8},{10,11... | collective-permute-start | bytes 1769480 | tf_op jit(solution)/shard_map/ppermute | solution.py:253
  521.8 9.9 %collective-permute-start.36 = (bf16[2,2,2,1,1,72,256]{6,5,4,3,2,1,0:T(8,128)(2,1)S(1)}, bf16[2,2,2,1,1,72,256]{6,5,4,3,2,1,0:T(8,128)(2,1)S(1)}, u32[]{:S(2)}, u32[]{:S(2)}) collective-permute-start(bf16[2,2,2,1,1,72,256]{6,5,4,3,2,1,0:T(8,128)(2,1)S(1)} %dynamic-slice_convert_fusion.11), channel_id=1, source_target_pairs={{0,2},{1,3},{2,0},{3,1},{4,6},{5,7},{6,4},{7,5},{8,10},{9,11},{10,... | collective-permute-start | bytes 884744 | tf_op jit(solution)/shard_map/ppermute | solution.py:253
  522.2 10.1 %collective-permute-start.41 = (bf16[2,2,1,2,1,72,256]{6,5,4,3,2,1,0:T(8,128)(2,1)S(1)}, bf16[2,2,1,2,1,72,256]{6,5,4,3,2,1,0:T(8,128)(2,1)S(1)}, u32[]{:S(2)}, u32[]{:S(2)}) collective-permute-start(bf16[2,2,1,2,1,72,256]{6,5,4,3,2,1,0:T(8,128)(2,1)S(1)} %dynamic-slice_convert_fusion.10), channel_id=1, source_target_pairs={{0,4},{1,5},{2,6},{3,7},{4,0},{5,1},{6,2},{7,3},{8,12},{9,13},{10,... | collective-permute-start | bytes 884744 | tf_op jit(solution)/shard_map/ppermute | solution.py:253
  524.1 9.9 %collective-permute-start.46 = (bf16[2,1,2,2,1,72,256]{6,5,4,3,2,1,0:T(8,128)(2,1)S(1)}, bf16[2,1,2,2,1,72,256]{6,5,4,3,2,1,0:T(8,128)(2,1)S(1)}, u32[]{:S(2)}, u32[]{:S(2)}) collective-permute-start(bf16[2,1,2,2,1,72,256]{6,5,4,3,2,1,0:T(8,128)(2,1)S(1)} %dynamic-slice_convert_fusion.9), channel_id=1, source_target_pairs={{0,8},{1,9},{2,10},{3,11},{4,12},{5,13},{6,14},{7,15},{8,0},{9,1},... | collective-permute-start | bytes 884744 | tf_op jit(solution)/shard_map/ppermute | solution.py:253
  526.1 11.1 %collective-permute-start.6 = (bf16[2,2,2,1,1,72,256]{6,5,4,3,2,1,0:T(8,128)(2,1)S(1)}, bf16[2,2,2,1,1,72,256]{6,5,4,3,2,1,0:T(8,128)(2,1)S(1)}, u32[]{:S(2)}, u32[]{:S(2)}) collective-permute-start(bf16[2,2,2,1,1,72,256]{6,5,4,3,2,1,0:T(8,128)(2,1)S(1)} %dynamic-slice_convert_fusion.14), channel_id=1, source_target_pairs={{0,2},{1,3},{2,0},{3,1},{4,6},{5,7},{6,4},{7,5},{8,10},{9,11},{10,... | collective-permute-start | bytes 884744 | tf_op jit(solution)/shard_map/ppermute | solution.py:253
  527.0 11.4 %collective-permute-start.11 = (bf16[2,2,1,2,1,72,256]{6,5,4,3,2,1,0:T(8,128)(2,1)S(1)}, bf16[2,2,1,2,1,72,256]{6,5,4,3,2,1,0:T(8,128)(2,1)S(1)}, u32[]{:S(2)}, u32[]{:S(2)}) collective-permute-start(bf16[2,2,1,2,1,72,256]{6,5,4,3,2,1,0:T(8,128)(2,1)S(1)} %dynamic-slice_convert_fusion.13), channel_id=1, source_target_pairs={{0,4},{1,5},{2,6},{3,7},{4,0},{5,1},{6,2},{7,3},{8,12},{9,13},{10,... | collective-permute-start | bytes 884744 | tf_op jit(solution)/shard_map/ppermute | solution.py:253
  531.8 8.8 %collective-permute-start.16 = (bf16[2,1,2,2,1,72,256]{6,5,4,3,2,1,0:T(8,128)(2,1)S(1)}, bf16[2,1,2,2,1,72,256]{6,5,4,3,2,1,0:T(8,128)(2,1)S(1)}, u32[]{:S(2)}, u32[]{:S(2)}) collective-permute-start(bf16[2,1,2,2,1,72,256]{6,5,4,3,2,1,0:T(8,128)(2,1)S(1)} %dynamic-slice_convert_fusion.12), channel_id=1, source_target_pairs={{0,8},{1,9},{2,10},{3,11},{4,12},{5,13},{6,14},{7,15},{8,0},{9,1},... | collective-permute-start | bytes 884744 | tf_op jit(solution)/shard_map/ppermute | solution.py:253
  532.3 9.9 %collective-permute-start.37 = (bf16[2,2,1,1,1,72,256]{6,5,4,3,2,1,0:T(8,128)(2,1)S(1)}, bf16[2,2,1,1,1,72,256]{6,5,4,3,2,1,0:T(8,128)(2,1)S(1)}, u32[]{:S(2)}, u32[]{:S(2)}) collective-permute-start(bf16[2,2,1,1,1,72,256]{6,5,4,3,2,1,0:T(8,128)(2,1)S(1)} %dynamic-slice_convert_fusion.23), channel_id=1, source_target_pairs={{0,4},{1,5},{2,6},{3,7},{4,0},{5,1},{6,2},{7,3},{8,12},{9,13},{10,... | collective-permute-start | bytes 442376 | tf_op jit(solution)/shard_map/ppermute | solution.py:253
  534.0 9.7 %collective-permute-start.42 = (bf16[2,1,1,2,1,72,256]{6,5,4,3,2,1,0:T(8,128)(2,1)S(1)}, bf16[2,1,1,2,1,72,256]{6,5,4,3,2,1,0:T(8,128)(2,1)S(1)}, u32[]{:S(2)}, u32[]{:S(2)}) collective-permute-start(bf16[2,1,1,2,1,72,256]{6,5,4,3,2,1,0:T(8,128)(2,1)S(1)} %dynamic-slice_convert_fusion.22), channel_id=1, source_target_pairs={{0,8},{1,9},{2,10},{3,11},{4,12},{5,13},{6,14},{7,15},{8,0},{9,1},... | collective-permute-start | bytes 442376 | tf_op jit(solution)/shard_map/ppermute | solution.py:253
  537.2 8.1 %collective-permute-start.47 = (bf16[2,1,2,1,1,72,256]{6,5,4,3,2,1,0:T(8,128)(2,1)S(1)}, bf16[2,1,2,1,1,72,256]{6,5,4,3,2,1,0:T(8,128)(2,1)S(1)}, u32[]{:S(2)}, u32[]{:S(2)}) collective-permute-start(bf16[2,1,2,1,1,72,256]{6,5,4,3,2,1,0:T(8,128)(2,1)S(1)} %dynamic-slice_convert_fusion.21), channel_id=1, source_target_pairs={{0,2},{1,3},{2,0},{3,1},{4,6},{5,7},{6,4},{7,5},{8,10},{9,11},{10,... | collective-permute-start | bytes 442376 | tf_op jit(solution)/shard_map/ppermute | solution.py:253
  538.4 7.7 %collective-permute-start.7 = (bf16[2,2,1,1,1,72,256]{6,5,4,3,2,1,0:T(8,128)(2,1)S(1)}, bf16[2,2,1,1,1,72,256]{6,5,4,3,2,1,0:T(8,128)(2,1)S(1)}, u32[]{:S(2)}, u32[]{:S(2)}) collective-permute-start(bf16[2,2,1,1,1,72,256]{6,5,4,3,2,1,0:T(8,128)(2,1)S(1)} %dynamic-slice_convert_fusion.26), channel_id=1, source_target_pairs={{0,4},{1,5},{2,6},{3,7},{4,0},{5,1},{6,2},{7,3},{8,12},{9,13},{10,... | collective-permute-start | bytes 442376 | tf_op jit(solution)/shard_map/ppermute | solution.py:253
  540.6 6.9 %collective-permute-start.12 = (bf16[2,1,1,2,1,72,256]{6,5,4,3,2,1,0:T(8,128)(2,1)S(1)}, bf16[2,1,1,2,1,72,256]{6,5,4,3,2,1,0:T(8,128)(2,1)S(1)}, u32[]{:S(2)}, u32[]{:S(2)}) collective-permute-start(bf16[2,1,1,2,1,72,256]{6,5,4,3,2,1,0:T(8,128)(2,1)S(1)} %dynamic-slice_convert_fusion.25), channel_id=1, source_target_pairs={{0,8},{1,9},{2,10},{3,11},{4,12},{5,13},{6,14},{7,15},{8,0},{9,1},... | collective-permute-start | bytes 442376 | tf_op jit(solution)/shard_map/ppermute | solution.py:253
  542.2 6.2 %collective-permute-start.17 = (bf16[2,1,2,1,1,72,256]{6,5,4,3,2,1,0:T(8,128)(2,1)S(1)}, bf16[2,1,2,1,1,72,256]{6,5,4,3,2,1,0:T(8,128)(2,1)S(1)}, u32[]{:S(2)}, u32[]{:S(2)}) collective-permute-start(bf16[2,1,2,1,1,72,256]{6,5,4,3,2,1,0:T(8,128)(2,1)S(1)} %dynamic-slice_convert_fusion.24), channel_id=1, source_target_pairs={{0,2},{1,3},{2,0},{3,1},{4,6},{5,7},{6,4},{7,5},{8,10},{9,11},{10,... | collective-permute-start | bytes 442376 | tf_op jit(solution)/shard_map/ppermute | solution.py:253
  547.5 6.5 %collective-permute-start.8 = (bf16[2,1,1,1,1,72,256]{6,5,4,3,2,1,0:T(8,128)(2,1)S(1)}, bf16[2,1,1,1,1,72,256]{6,5,4,3,2,1,0:T(8,128)(2,1)S(1)}, u32[]{:S(2)}, u32[]{:S(2)}) collective-permute-start(bf16[2,1,1,1,1,72,256]{6,5,4,3,2,1,0:T(8,128)(2,1)S(1)} %dynamic-slice_convert_fusion.38), channel_id=1, source_target_pairs={{0,8},{1,9},{2,10},{3,11},{4,12},{5,13},{6,14},{7,15},{8,0},{9,1},... | collective-permute-start | bytes 221192 | tf_op jit(solution)/shard_map/ppermute | solution.py:253
  549.6 7.6 %collective-permute-start.18 = (bf16[2,1,1,1,1,72,256]{6,5,4,3,2,1,0:T(8,128)(2,1)S(1)}, bf16[2,1,1,1,1,72,256]{6,5,4,3,2,1,0:T(8,128)(2,1)S(1)}, u32[]{:S(2)}, u32[]{:S(2)}) collective-permute-start(bf16[2,1,1,1,1,72,256]{6,5,4,3,2,1,0:T(8,128)(2,1)S(1)} %dynamic-slice_convert_fusion.36), channel_id=1, source_target_pairs={{0,4},{1,5},{2,6},{3,7},{4,0},{5,1},{6,2},{7,3},{8,12},{9,13},{10,... | collective-permute-start | bytes 221192 | tf_op jit(solution)/shard_map/ppermute | solution.py:253
  550.8 6.8 %collective-permute-start.39 = (bf16[1,1,1,1,1,72,256]{6,5,4,3,2,1,0:T(8,128)(2,1)S(1)}, bf16[1,1,1,1,1,72,256]{6,5,4,3,2,1,0:T(8,128)(2,1)S(1)}, u32[]{:S(2)}, u32[]{:S(2)}) collective-permute-start(bf16[1,1,1,1,1,72,256]{6,5,4,3,2,1,0:T(8,128)(2,1)S(1)} %dynamic-slice_convert_fusion.47), channel_id=1, source_target_pairs={{0,16},{1,17},{2,18},{3,19},{4,20},{5,21},{6,22},{7,23},{8,24},{9,... | collective-permute-start | bytes 110600 | tf_op jit(solution)/shard_map/ppermute | solution.py:253
  551.0 9.3 %collective-permute-start.44 = (bf16[1,1,1,1,1,72,256]{6,5,4,3,2,1,0:T(8,128)(2,1)S(1)}, bf16[1,1,1,1,1,72,256]{6,5,4,3,2,1,0:T(8,128)(2,1)S(1)}, u32[]{:S(2)}, u32[]{:S(2)}) collective-permute-start(bf16[1,1,1,1,1,72,256]{6,5,4,3,2,1,0:T(8,128)(2,1)S(1)} %dynamic-slice_convert_fusion.46), channel_id=1, source_target_pairs={{0,16},{1,17},{2,18},{3,19},{4,20},{5,21},{6,22},{7,23},{8,24},{9,... | collective-permute-start | bytes 110600 | tf_op jit(solution)/shard_map/ppermute | solution.py:253
  554.0 6.3 %collective-permute-start.49 = (bf16[1,1,1,1,1,72,256]{6,5,4,3,2,1,0:T(8,128)(2,1)S(1)}, bf16[1,1,1,1,1,72,256]{6,5,4,3,2,1,0:T(8,128)(2,1)S(1)}, u32[]{:S(2)}, u32[]{:S(2)}) collective-permute-start(bf16[1,1,1,1,1,72,256]{6,5,4,3,2,1,0:T(8,128)(2,1)S(1)} %dynamic-slice_convert_fusion.45), channel_id=1, source_target_pairs={{0,16},{1,17},{2,18},{3,19},{4,20},{5,21},{6,22},{7,23},{8,24},{9,... | collective-permute-start | bytes 110600 | tf_op jit(solution)/shard_map/ppermute | solution.py:253
  (107 other events, 1057.4 us)
Sparse Core Ops, SparseCore 0:
  10.9 62.7 all-gather.4
  76.7 52.9 all-gather.6
  132.6 59.0 all-gather.8
  194.3 54.4 all-gather.10

commit v2 on v1

--- a/solution.py
+++ b/solution.py
@@ -276,15 +276,22 @@
 
 def doubling_gather(block, device_count):
     me = lax.axis_index("fsdp")
-    current = block
-    for bit in range(device_count.bit_length() - 1):
+    bits = device_count.bit_length() - 1
+    current = block[0]
+    for stage in range(bits):
+        bit = bits - 1 - stage
         pairs = [(index, index ^ (1 << bit)) for index in range(device_count)]
         other = lax.ppermute(current, "fsdp", pairs)
         upper = (me >> bit) & 1 == 1
-        current = jnp.concatenate(
-            [jnp.where(upper, other, current), jnp.where(upper, current, other)], axis=0
+        current = jnp.stack(
+            [jnp.where(upper, other, current), jnp.where(upper, current, other)], axis=stage
         )
-    return current
+    return current.reshape((device_count,) + block.shape[1:])
+
+
+def full_rows(block, device_count):
+    gathered = doubling_gather(block[None], device_count)
+    return gathered.reshape(device_count * block.shape[0], block.shape[1])
 
 
 def gains_to_owners(gain_one, gain_two, device_count):
@@ -325,10 +332,10 @@
     gains = doubling_gather(both_gains[None], device_count)
     gain_one = gains[:, 0, :own_gain].reshape(device_count * own_gain)
     gain_two = gains[:, 1, :own_gain].reshape(device_count * own_gain)
-    full_in = lax.all_gather(project_in, "fsdp", axis=0, tiled=True)
-    full_out = lax.all_gather(project_out, "fsdp", axis=0, tiled=True)
-    full_expand = lax.all_gather(expand_weight, "fsdp", axis=0, tiled=True)
-    full_shrink = lax.all_gather(shrink_weight, "fsdp", axis=0, tiled=True)
+    full_in = full_rows(project_in, device_count)
+    full_out = full_rows(project_out, device_count)
+    full_expand = full_rows(expand_weight, device_count)
+    full_shrink = full_rows(shrink_weight, device_count)
     tables = attention_tables(segment_ids)
     hidden = hidden_in.astype(jnp.float32)
     normed, norm_back_one = jax.vjp(layer_norm, hidden, gain_one.astype(jnp.float32))

time: 582 us -> 494 us (0.85)
  waiting for transfers between devices: 268 us -> 164 us
  starting transfers between devices: 55.2 us -> 82.2 us
  other arithmetic: 26.6 us -> 44.2 us
  matrix products: 81.7 us -> 65.9 us
  between operations: 16 us -> 3.33 us
    all_gather x4 -> x0, waiting for transfers between devices: 145 us -> none  [the longest x1 54.8 us: local(): full_expand = lax.all_gather(expand_weight, 'fsdp', axis=0, tiled=True)]
    ppermute x5 -> x25, waiting for transfers between devices: 4.05 us -> 52.5 us  [doubling_gather(): other = lax.ppermute(current, 'fsdp', pairs)]
    another operation x1 -> x51, other arithmetic: 2.76 us -> 23 us  [the longest x49 13.8 us: doubling_gather(): jnp.stack([jnp.where(upper, other, current), jnp.where(upper, current, ot...]
    ppermute x5 -> x25, starting transfers between devices: 10.4 us -> 27.6 us  [doubling_gather(): other = lax.ppermute(current, 'fsdp', pairs)]
    dot_general x4, matrix products: 30 us -> 16 us  [right_product(): lax.dot_general(left, weight, (((1,), (1,)), ((), ())), preferred_element...]
    ppermute x65, starting transfers between devices: 44.6 us -> 54.6 us  [halving_sum(): current = keep + lax.ppermute(send, 'fsdp', pairs).astype(jnp.float32)]
    unnamed x137 -> x165, local copies, waits for them, and re-layouts: 23.4 us -> 18.9 us
  transfers between devices with their start and end apart: 74 -> 90, of which waited for: 44 -> 51; matrix products, arithmetic and copies ran while one was open for 13% -> 14% of each run, Pallas kernels for 7% -> 8%
where the time goes in v2:
time: 494 us; the launch traced here: 485 us
  waiting for transfers between devices  164 us (33%)
  Pallas kernels  86.6 us (18%)
  starting transfers between devices  82.2 us (17%)
  matrix products  65.9 us (13%)
  other arithmetic  44.2 us (9%)
  local copies, waits for them, and re-layouts  38.5 us (8%)
    ppermute x65, waiting for transfers between devices, halving_sum(): current = keep + lax.ppermute(send, 'fsdp', pairs).astype(jnp.float32)  112 us
    ppermute x65, starting transfers between devices, halving_sum(): current = keep + lax.ppermute(send, 'fsdp', pairs).astype(jnp.float32)  54.6 us
    ppermute x25, waiting for transfers between devices, doubling_gather(): other = lax.ppermute(current, 'fsdp', pairs)  52.5 us
    pallas_call x1, Pallas kernels, attend_back(): pl.pallas_call(attend_back_kernel, grid_spec=pltpu.PrefetchScalarGridSpec...  47.6 us
    pallas_call x1, Pallas kernels, attend(): pl.pallas_call(attend_kernel, grid_spec=pltpu.PrefetchScalarGridSpec(num_...  39 us
    ppermute x25, starting transfers between devices, doubling_gather(): other = lax.ppermute(current, 'fsdp', pairs)  27.6 us
    dot_general x4, matrix products, outer_sum(): lax.dot_general(grads, inputs, (((0,), (0,)), ((), ())), preferred_elemen...  20.5 us
    unnamed x165, local copies, waits for them, and re-layouts  18.9 us
  transfers between devices with their start and end apart: 90, of which 51 were waited for; matrix products, arithmetic and copies ran while one was open for 14% of the time, Pallas kernels for 8%

profile of v2, /device:TPU:0, one launch (start us, length us, event | category | flops | bytes accessed | tf_op | source)
XLA Modules:
  0.0 485.2 jit_solution(6753732296996795928)
XLA Ops:
  0.7 4.1 collective-permute-start.20
  55.0 7.2 %collective-permute-done.7 = bf16[2,2,72,768]{3,2,1,0:T(8,128)(2,1)S(1)} collective-permute-done((bf16[2,2,72,768]{3,2,1,0:T(8,128)(2,1)S(1)}, bf16[2,2,72,768]{3,2,1,0:T(8,128)(2,1)S(1)}, u32[]{:S(2)}, u32[]{:S(2)}) %collective-permute-start.7) | collective-permute-done | bytes 442400 | tf_op jit(solution)/shard_map/ppermute | solution.py:284
  71.7 13.3 %collective-permute-done.8 = bf16[2,2,2,72,768]{4,3,2,1,0:T(8,128)(2,1)S(1)} collective-permute-done((bf16[2,2,2,72,768]{4,3,2,1,0:T(8,128)(2,1)S(1)}, bf16[2,2,2,72,768]{4,3,2,1,0:T(8,128)(2,1)S(1)}, u32[]{:S(2)}, u32[]{:S(2)}) %collective-permute-start.8) | collective-permute-done | bytes 884768 | tf_op jit(solution)/shard_map/ppermute | solution.py:284
  89.2 11.1 %collective-permute-done.18 = bf16[2,2,2,72,768]{4,3,0,1,2:T(8,128)(2,1)} collective-permute-done((bf16[2,2,2,72,768]{4,3,0,1,2:T(8,128)(2,1)}, bf16[2,2,2,72,768]{4,3,0,1,2:T(8,128)(2,1)}, u32[]{:S(2)}, u32[]{:S(2)}) %collective-permute-start.18) | collective-permute-done | bytes 884768 | tf_op jit(solution)/shard_map/ppermute | solution.py:284
  106.8 7.0 %fusion.27.q_ref.k_ref.v_ref = f32[1024,2304]{1,0:T(8,128)} fusion(bf16[2304,768]{1,0:T(8,128)(2,1)S(1)} %bitcast.225, bf16[1024,768]{0,1:T(8,128)(2,1)S(1)} %copy.51, f32[768]{0:T(1024)S(1)} %reshape.225, f32[1024]{0:T(1024)S(1)} %copy-done.67, f32[1024]{0:T(1024)S(1)} %broadcast_multiply_fusion.1), kind=kOutput, calls=%fused_computation.147 | convolution fusion | flops 3627810816 | bytes 14560256 | tf_op jit(solution)/shard_map/dot_general | solution.py:306
  114.0 39.0 %shard_map.152 = (bf16[1024,768]{1,0:T(8,128)(2,1)S(1)}, bf16[1024,768]{1,0:T(8,128)(2,1)S(1)}, bf16[1024,768]{1,0:T(8,128)(2,1)S(1)}, bf16[1024,768]{1,0:T(8,128)(2,1)S(1)}, f32[6,8,1024]{2,1,0:T(8,128)S(1)}) custom-call(s32[4]{0:T(128)S(1)} %get-tuple-element.58.lo_ref, s32[4]{0:T(128)S(1)} %get-tuple-element.59.width_ref, ...), custom_call_target="tpu_custom_call" | custom-call | flops 12884901888 | bytes 18874368 | tf_op jit(solution)/shard_map/pallas_call | solution.py:190
  155.8 4.2 fusion.64
  160.0 15.0 %add_convert_fusion = (bf16[1024,1152]{1,0:T(8,128)(2,1)}, f32[1024,1152]{1,0:T(8,128)S(1)}, f32[1152,1024]{0,1:T(8,128)}) fusion(f32[1024,2304]{1,0:T(8,128)S(1)} %fusion.64, bf16[1024,768]{1,0:T(8,128)(2,1)S(1)} %copy-done.51, bf16[768,1152]{1,0:T(8,128)(2,1)S(1)} %bitcast.235), kind=kOutput, calls=%fused_computation.17 | convolution fusion | flops 1898053632 | bytes 24576000 | tf_op jit(solution)/shard_map/dot_general | solution.py:353
  175.0 8.6 %fusion.5 = (bf16[1024,1152]{1,0:T(8,128)(2,1)}, bf16[1024,1152]{1,0:T(8,128)(2,1)}) fusion(f32[1152,1024]{0,1:T(8,128)} %get-tuple-element.138, f32[1024,1152]{1,0:T(8,128)S(1)} %get-tuple-element.57, f32[1024,2304]{1,0:T(8,128)} %copy-done.6), kind=kLoop, calls=%fused_computation.16 | loop fusion | flops 7077888 | bytes 23592960 | tf_op jit(solution)/shard_map/convert.3
  183.6 8.8 %multiply_reduce_fusion = (f32[768]{0:T(1024)S(1)}, f32[1024]{0:T(1024)S(1)}, f32[1024,768]{0,1:T(8,128)}) fusion(f32[1024,768]{0,1:T(8,128)S(1)} %get-tuple-element.137, f32[1024]{0:T(1024)S(1)} %fusion.45, f32[1024]{0:T(1024)S(1)} %broadcast_multiply_fusion, f32[768]{0:T(1024)S(1)} %reshape.226, bf16[2304,768]{1,0:T(8,128)(2,1)S(1)} %bitcast.228, ...), kind=kOutput, calls=%fused_computation.45 | convolution fusion | flops 3638819072 | bytes 14567424 | tf_op jit(solution)/shard_map/dot_general | solution.py:357
  192.4 7.2 %fusion.20 = f32[2304,768]{1,0:T(8,128)} fusion(bf16[1024,1152]{1,0:T(8,128)(2,1)S(1)} %copy-done.47, bf16[1024,1152]{1,0:T(8,128)(2,1)S(1)} %copy-done.76, f32[1024,768]{0,1:T(8,128)S(1)} %get-tuple-element.137, f32[768]{0:T(1024)S(1)} %reshape.226, f32[1024]{0:T(1024)S(1)} %fusion.45, f32[1024]{0:T(1024)S(1)} %broadcast_multiply_fusion), kind=kOutput, calls=%fused_computation.52 | convolution fusion | flops 3636461568 | bytes 14953472 | tf_op jit(solution)/shard_map/dot_general | solution.py:312
  207.0 47.6 %shard_map.153 = (bf16[1024,768]{1,0:T(8,128)(2,1)S(1)}, bf16[1024,768]{1,0:T(8,128)(2,1)S(1)}, bf16[1024,768]{1,0:T(8,128)(2,1)S(1)}) custom-call(s32[4]{0:T(128)S(1)} %get-tuple-element.58.lo_ref, s32[4]{0:T(128)S(1)} %get-tuple-element.59.width_ref, bf16[1024,768]{1,0:T(8,128)(2,1)S(1)} %get-tuple-element.17.qr_ref, ...), custom_call_target="tpu_custom_call" | custom-call | flops 32212254720 | bytes 15728640 | tf_op jit(solution)/shard_map/pallas_call | solution.py:219
  256.8 4.2 fusion.19
  261.1 6.5 %fusion.25 = f32[2304,768]{1,0:T(8,128)} fusion(bf16[1024,2304]{1,0:T(8,128)(2,1)S(1)} %constant_dynamic-update-slice_fusion, bf16[1024,768]{0,1:T(8,128)(2,1)S(1)} %copy.51, f32[768]{0:T(1024)S(1)} %copy-done.66, f32[1024]{0:T(1024)S(1)} %copy-done.68, f32[1024]{0:T(1024)S(1)} %copy-done.63), kind=kOutput, calls=%fused_computation.146 | convolution fusion | flops 3627810816 | bytes 13380608 | tf_op jit(solution)/shard_map/dot_general | solution.py:312
  267.6 4.0 convolution_bitcast_fusion
  299.5 5.4 %collective-permute-start.86 = (f32[2,2,2,1,1,2,128]{6,5,4,3,2,1,0:T(2,128)S(1)}, f32[2,2,2,1,1,2,128]{6,5,4,3,2,1,0:T(2,128)S(1)}, u32[]{:S(2)}, u32[]{:S(2)}) collective-permute-start(f32[2,2,2,1,1,2,128]{6,5,4,3,2,1,0:T(2,128)S(1)} %constant_dynamic-slice_fusion.6), channel_id=1, source_target_pairs={{0,2},{1,3},{2,0},{3,1},{4,6},{5,7},{6,4},{7,5},{8,10},{9,11},{10,... | collective-permute-start | bytes 24584 | tf_op jit(solution)/shard_map/ppermute | solution.py:253
  314.6 7.0 %collective-permute-start.89 = (f32[1,1,1,1,1,2,128]{6,5,4,3,2,1,0:T(2,128)S(1)}, f32[1,1,1,1,1,2,128]{6,5,4,3,2,1,0:T(2,128)S(1)}, u32[]{:S(2)}, u32[]{:S(2)}) collective-permute-start(f32[1,1,1,1,1,2,128]{6,5,4,3,2,1,0:T(2,128)S(1)} %constant_dynamic-slice_fusion), channel_id=1, source_target_pairs={{0,16},{1,17},{2,18},{3,19},{4,20},{5,21},{6,22},{7,23},{8,24},{9,... | collective-permute-start | bytes 3080 | tf_op jit(solution)/shard_map/ppermute | solution.py:253
  339.0 4.6 collective-permute-done.46
  343.6 4.6 collective-permute-done.51
  348.2 4.0 collective-permute-done.42
  352.3 4.0 collective-permute-done.47
  372.2 4.3 collective-permute-done.44
  376.8 4.3 collective-permute-done.49
  381.4 4.3 collective-permute-done.54
  391.2 4.8 collective-permute-done.76
  396.3 4.8 collective-permute-done.81
  401.5 4.0 collective-permute-done.72
  405.8 4.0 collective-permute-done.77
  426.5 4.3 collective-permute-done.74
  431.1 4.3 collective-permute-done.79
  435.8 4.3 collective-permute-done.84
  448.6 4.1 collective-permute-done.56
  (551 shorter events, 217.1 us)
Async XLA Ops:
  0.7 33.3 %collective-permute-start.20 = (bf16[24,1152]{1,0:T(8,128)(2,1)}, bf16[24,1152]{1,0:T(8,128)(2,1)S(1)}, u32[]{:S(2)}, u32[]{:S(2)}) collective-permute-start(bf16[24,1152]{1,0:T(8,128)(2,1)} %param.14), channel_id=1, source_target_pairs={{0,16},{1,17},{2,18},{3,19},{4,20},{5,21},{6,22},{7,23},{8,24},{9,... | collective-permute-start | bytes 165896 | tf_op jit(solution)/shard_map/ppermute | solution.py:284
  4.8 28.8 %collective-permute-start.10 = (bf16[24,768]{1,0:T(8,128)(2,1)}, bf16[24,768]{1,0:T(8,128)(2,1)S(1)}, u32[]{:S(2)}, u32[]{:S(2)}) collective-permute-start(bf16[24,768]{1,0:T(8,128)(2,1)} %param.12), channel_id=1, source_target_pairs={{0,16},{1,17},{2,18},{3,19},{4,20},{5,21},{6,22},{7,23},{8,24},{9,... | collective-permute-start | bytes 110600 | tf_op jit(solution)/shard_map/ppermute | solution.py:284
  4.8 35.5 %collective-permute-start.15 = (bf16[72,768]{1,0:T(8,128)(2,1)}, bf16[72,768]{1,0:T(8,128)(2,1)S(1)}, u32[]{:S(2)}, u32[]{:S(2)}) collective-permute-start(bf16[72,768]{1,0:T(8,128)(2,1)} %param.13), channel_id=1, source_target_pairs={{0,16},{1,17},{2,18},{3,19},{4,20},{5,21},{6,22},{7,23},{8,24},{9,... | collective-permute-start | bytes 331784 | tf_op jit(solution)/shard_map/ppermute | solution.py:284
  7.7 32.7 %collective-permute-start.5 = (bf16[72,768]{1,0:T(8,128)(2,1)}, bf16[72,768]{1,0:T(8,128)(2,1)S(1)}, u32[]{:S(2)}, u32[]{:S(2)}) collective-permute-start(bf16[72,768]{1,0:T(8,128)(2,1)} %param.11), channel_id=1, source_target_pairs={{0,16},{1,17},{2,18},{3,19},{4,20},{5,21},{6,22},{7,23},{8,24},{9,... | collective-permute-start | bytes 331784 | tf_op jit(solution)/shard_map/ppermute | solution.py:284
  8.5 11.1 %collective-permute-start = (bf16[2,128]{1,0:T(2,128)(2,1)S(1)}, bf16[2,128]{1,0:T(2,128)(2,1)S(1)}, u32[]{:S(2)}, u32[]{:S(2)}) collective-permute-start(bf16[2,128]{1,0:T(2,128)(2,1)S(1)} %fusion.57), channel_id=1, source_target_pairs={{0,16},{1,17},{2,18},{3,19},{4,20},{5,21},{6,22},{7,23},{8,24},{9,... | collective-permute-start | bytes 1544 | tf_op jit(solution)/shard_map/ppermute | solution.py:284
  40.6 11.1 %collective-permute-start.16 = (bf16[2,72,768]{2,1,0:T(8,128)(2,1)S(1)}, bf16[2,72,768]{2,1,0:T(8,128)(2,1)S(1)}, u32[]{:S(2)}, u32[]{:S(2)}) collective-permute-start(bf16[2,72,768]{2,1,0:T(8,128)(2,1)S(1)} %pad_maximum_fusion.18), channel_id=1, source_target_pairs={{0,8},{1,9},{2,10},{3,11},{4,12},{5,13},{6,14},{7,15},{8,0},{9,1},... | collective-permute-start | bytes 663560 | tf_op jit(solution)/shard_map/ppermute | solution.py:284
  42.7 9.5 %collective-permute-start.22 = (bf16[2,2,24,1152]{3,2,1,0:T(8,128)(2,1)S(1)}, bf16[2,2,24,1152]{3,2,1,0:T(8,128)(2,1)S(1)}, u32[]{:S(2)}, u32[]{:S(2)}) collective-permute-start(bf16[2,2,24,1152]{3,2,1,0:T(8,128)(2,1)S(1)} %pad_maximum_fusion.19), channel_id=1, source_target_pairs={{0,4},{1,5},{2,6},{3,7},{4,0},{5,1},{6,2},{7,3},{8,12},{9,13},{10,... | collective-permute-start | bytes 663560 | tf_op jit(solution)/shard_map/ppermute | solution.py:284
  44.1 9.9 %collective-permute-start.13 = (bf16[2,2,2,24,768]{4,3,2,1,0:T(8,128)(2,1)S(1)}, bf16[2,2,2,24,768]{4,3,2,1,0:T(8,128)(2,1)S(1)}, u32[]{:S(2)}, u32[]{:S(2)}) collective-permute-start(bf16[2,2,2,24,768]{4,3,2,1,0:T(8,128)(2,1)S(1)} %pad_maximum_fusion.16), channel_id=1, source_target_pairs={{0,2},{1,3},{2,0},{3,1},{4,6},{5,7},{6,4},{7,5},{8,10},{9,11},{10,... | collective-permute-start | bytes 884744 | tf_op jit(solution)/shard_map/ppermute | solution.py:284
  49.0 13.2 %collective-permute-start.7 = (bf16[2,2,72,768]{3,2,1,0:T(8,128)(2,1)S(1)}, bf16[2,2,72,768]{3,2,1,0:T(8,128)(2,1)S(1)}, u32[]{:S(2)}, u32[]{:S(2)}) collective-permute-start(bf16[2,2,72,768]{3,2,1,0:T(8,128)(2,1)S(1)} %pad_maximum_fusion.13), channel_id=1, source_target_pairs={{0,4},{1,5},{2,6},{3,7},{4,0},{5,1},{6,2},{7,3},{8,12},{9,13},{10,... | collective-permute-start | bytes 1327112 | tf_op jit(solution)/shard_map/ppermute | solution.py:284
  51.7 16.0 %collective-permute-start.17 = (bf16[2,2,72,768]{3,2,0,1:T(8,128)(2,1)S(1)}, bf16[2,2,72,768]{3,2,0,1:T(8,128)(2,1)S(1)}, u32[]{:S(2)}, u32[]{:S(2)}) collective-permute-start(bf16[2,2,72,768]{3,2,0,1:T(8,128)(2,1)S(1)} %pad_maximum_fusion.14), channel_id=1, source_target_pairs={{0,4},{1,5},{2,6},{3,7},{4,0},{5,1},{6,2},{7,3},{8,12},{9,13},{10,... | collective-permute-start | bytes 1327112 | tf_op jit(solution)/shard_map/ppermute | solution.py:284
  52.4 18.0 %collective-permute-start.23 = (bf16[2,2,2,24,1152]{4,3,2,1,0:T(8,128)(2,1)S(1)}, bf16[2,2,2,24,1152]{4,3,2,1,0:T(8,128)(2,1)S(1)}, u32[]{:S(2)}, u32[]{:S(2)}) collective-permute-start(bf16[2,2,2,24,1152]{4,3,2,1,0:T(8,128)(2,1)S(1)} %pad_maximum_fusion.15), channel_id=1, source_target_pairs={{0,2},{1,3},{2,0},{3,1},{4,6},{5,7},{6,4},{7,5},{8,10},{9,11},{10,... | collective-permute-start | bytes 1327112 | tf_op jit(solution)/shard_map/ppermute | solution.py:284
  55.0 32.7 %collective-permute-start.14 = (bf16[2,2,2,2,24,768]{5,4,3,2,1,0:T(8,128)(2,1)}, bf16[2,2,2,2,24,768]{5,4,3,2,1,0:T(8,128)(2,1)}, u32[]{:S(2)}, u32[]{:S(2)}) collective-permute-start(bf16[2,2,2,2,24,768]{5,4,3,2,1,0:T(8,128)(2,1)} %pad_maximum_fusion.12), channel_id=1, source_target_pairs={{0,1},{1,0},{2,3},{3,2},{4,5},{5,4},{6,7},{7,6},{8,9},{9,8},{10,11... | collective-permute-start | bytes 1769480 | tf_op jit(solution)/shard_map/ppermute | solution.py:284
  62.4 22.7 %collective-permute-start.8 = (bf16[2,2,2,72,768]{4,3,2,1,0:T(8,128)(2,1)S(1)}, bf16[2,2,2,72,768]{4,3,2,1,0:T(8,128)(2,1)S(1)}, u32[]{:S(2)}, u32[]{:S(2)}) collective-permute-start(bf16[2,2,2,72,768]{4,3,2,1,0:T(8,128)(2,1)S(1)} %pad_maximum_fusion.9), channel_id=1, source_target_pairs={{0,2},{1,3},{2,0},{3,1},{4,6},{5,7},{6,4},{7,5},{8,10},{9,11},{10,... | collective-permute-start | bytes 2654216 | tf_op jit(solution)/shard_map/ppermute | solution.py:284
  68.9 31.5 %collective-permute-start.18 = (bf16[2,2,2,72,768]{4,3,0,1,2:T(8,128)(2,1)}, bf16[2,2,2,72,768]{4,3,0,1,2:T(8,128)(2,1)}, u32[]{:S(2)}, u32[]{:S(2)}) collective-permute-start(bf16[2,2,2,72,768]{4,3,0,1,2:T(8,128)(2,1)} %pad_maximum_fusion.10), channel_id=1, source_target_pairs={{0,2},{1,3},{2,0},{3,1},{4,6},{5,7},{6,4},{7,5},{8,10},{9,11},{10,... | collective-permute-start | bytes 2654216 | tf_op jit(solution)/shard_map/ppermute | solution.py:284
  71.7 30.3 %collective-permute-start.24 = (bf16[2,2,2,2,24,1152]{5,4,3,2,1,0:T(8,128)(2,1)}, bf16[2,2,2,2,24,1152]{5,4,3,2,1,0:T(8,128)(2,1)}, u32[]{:S(2)}, u32[]{:S(2)}) collective-permute-start(bf16[2,2,2,2,24,1152]{5,4,3,2,1,0:T(8,128)(2,1)} %pad_maximum_fusion.11), channel_id=1, source_target_pairs={{0,1},{1,0},{2,3},{3,2},{4,5},{5,4},{6,7},{7,6},{8,9},{9,8},{10,11... | collective-permute-start | bytes 2654216 | tf_op jit(solution)/shard_map/ppermute | solution.py:284
  87.5 16.2 %collective-permute-start.9 = (bf16[2,2,2,2,72,768]{5,4,3,2,1,0:T(8,128)(2,1)}, bf16[2,2,2,2,72,768]{5,4,3,2,1,0:T(8,128)(2,1)}, u32[]{:S(2)}, u32[]{:S(2)}) collective-permute-start(bf16[2,2,2,2,72,768]{5,4,3,2,1,0:T(8,128)(2,1)} %pad_maximum_fusion.5), channel_id=1, source_target_pairs={{0,1},{1,0},{2,3},{3,2},{4,5},{5,4},{6,7},{7,6},{8,9},{9,8},{10,11... | collective-permute-start | bytes 5308424 | tf_op jit(solution)/shard_map/ppermute | solution.py:284
  102.0 52.9 %collective-permute-start.19 = (bf16[2,2,2,2,72,768]{5,4,0,1,2,3:T(8,128)(2,1)S(1)}, bf16[2,2,2,2,72,768]{5,4,0,1,2,3:T(8,128)(2,1)S(1)}, u32[]{:S(2)}, u32[]{:S(2)}) collective-permute-start(bf16[2,2,2,2,72,768]{5,4,0,1,2,3:T(8,128)(2,1)S(1)} %pad_maximum_fusion.6), channel_id=1, source_target_pairs={{0,1},{1,0},{2,3},{3,2},{4,5},{5,4},{6,7},{7,6},{8,9},{9,8},{10,11... | collective-permute-start | bytes 5308424 | tf_op jit(solution)/shard_map/ppermute | solution.py:284
  276.5 22.9 %collective-permute-start.85 = (f32[2,2,2,2,1,2,128]{6,5,4,3,2,1,0:T(2,128)S(1)}, f32[2,2,2,2,1,2,128]{6,5,4,3,2,1,0:T(2,128)S(1)}, u32[]{:S(2)}, u32[]{:S(2)}) collective-permute-start(f32[2,2,2,2,1,2,128]{6,5,4,3,2,1,0:T(2,128)S(1)} %copy.82), channel_id=1, source_target_pairs={{0,1},{1,0},{2,3},{3,2},{4,5},{5,4},{6,7},{7,6},{8,9},{9,8},{10,11... | collective-permute-start | bytes 49160 | tf_op jit(solution)/shard_map/ppermute | solution.py:253
  279.7 51.3 %collective-permute-start.70 = (bf16[2,2,2,2,1,24,384]{6,5,4,3,2,1,0:T(8,128)(2,1)}, bf16[2,2,2,2,1,24,384]{6,5,4,3,2,1,0:T(8,128)(2,1)}, u32[]{:S(2)}, u32[]{:S(2)}) collective-permute-start(bf16[2,2,2,2,1,24,384]{6,5,4,3,2,1,0:T(8,128)(2,1)} %dynamic-slice_convert_fusion.8), channel_id=1, source_target_pairs={{0,1},{1,0},{2,3},{3,2},{4,5},{5,4},{6,7},{7,6},{8,9},{9,8},{10,11... | collective-permute-start | bytes 884744 | tf_op jit(solution)/shard_map/ppermute | solution.py:253
  281.0 51.5 %collective-permute-start.75 = (bf16[2,2,2,2,1,24,384]{6,5,4,3,2,1,0:T(8,128)(2,1)}, bf16[2,2,2,2,1,24,384]{6,5,4,3,2,1,0:T(8,128)(2,1)}, u32[]{:S(2)}, u32[]{:S(2)}) collective-permute-start(bf16[2,2,2,2,1,24,384]{6,5,4,3,2,1,0:T(8,128)(2,1)} %dynamic-slice_convert_fusion.7), channel_id=1, source_target_pairs={{0,1},{1,0},{2,3},{3,2},{4,5},{5,4},{6,7},{7,6},{8,9},{9,8},{10,11... | collective-permute-start | bytes 884744 | tf_op jit(solution)/shard_map/ppermute | solution.py:253
  281.8 52.0 %collective-permute-start.80 = (bf16[2,2,2,2,1,24,384]{6,5,4,3,2,1,0:T(8,128)(2,1)}, bf16[2,2,2,2,1,24,384]{6,5,4,3,2,1,0:T(8,128)(2,1)}, u32[]{:S(2)}, u32[]{:S(2)}) collective-permute-start(bf16[2,2,2,2,1,24,384]{6,5,4,3,2,1,0:T(8,128)(2,1)} %dynamic-slice_convert_fusion.6), channel_id=1, source_target_pairs={{0,1},{1,0},{2,3},{3,2},{4,5},{5,4},{6,7},{7,6},{8,9},{9,8},{10,11... | collective-permute-start | bytes 884744 | tf_op jit(solution)/shard_map/ppermute | solution.py:253
  287.1 153.7 %collective-permute-start.55 = (bf16[2,2,2,2,1,72,256]{6,5,4,3,2,1,0:T(8,128)(2,1)}, bf16[2,2,2,2,1,72,256]{6,5,4,3,2,1,0:T(8,128)(2,1)}, u32[]{:S(2)}, u32[]{:S(2)}) collective-permute-start(bf16[2,2,2,2,1,72,256]{6,5,4,3,2,1,0:T(8,128)(2,1)} %dynamic-slice_convert_fusion.2), channel_id=1, source_target_pairs={{0,1},{1,0},{2,3},{3,2},{4,5},{5,4},{6,7},{7,6},{8,9},{9,8},{10,11... | collective-permute-start | bytes 1769480 | tf_op jit(solution)/shard_map/ppermute | solution.py:253
  314.6 11.1 %collective-permute-start.89 = (f32[1,1,1,1,1,2,128]{6,5,4,3,2,1,0:T(2,128)S(1)}, f32[1,1,1,1,1,2,128]{6,5,4,3,2,1,0:T(2,128)S(1)}, u32[]{:S(2)}, u32[]{:S(2)}) collective-permute-start(f32[1,1,1,1,1,2,128]{6,5,4,3,2,1,0:T(2,128)S(1)} %constant_dynamic-slice_fusion), channel_id=1, source_target_pairs={{0,16},{1,17},{2,18},{3,19},{4,20},{5,21},{6,22},{7,23},{8,24},{9,... | collective-permute-start | bytes 3080 | tf_op jit(solution)/shard_map/ppermute | solution.py:253
  330.7 112.1 %collective-permute-start.60 = (bf16[2,2,2,2,1,72,256]{6,5,4,3,2,1,0:T(8,128)(2,1)}, bf16[2,2,2,2,1,72,256]{6,5,4,3,2,1,0:T(8,128)(2,1)S(1)}, u32[]{:S(2)}, u32[]{:S(2)}) collective-permute-start(bf16[2,2,2,2,1,72,256]{6,5,4,3,2,1,0:T(8,128)(2,1)} %dynamic-slice_convert_fusion.1), channel_id=1, source_target_pairs={{0,1},{1,0},{2,3},{3,2},{4,5},{5,4},{6,7},{7,6},{8,9},{9,8},{10,11... | collective-permute-start | bytes 1769480 | tf_op jit(solution)/shard_map/ppermute | solution.py:253
  331.0 113.4 %collective-permute-start.65 = (bf16[2,2,2,2,1,72,256]{6,5,4,3,2,1,0:T(8,128)(2,1)S(1)}, bf16[2,2,2,2,1,72,256]{6,5,4,3,2,1,0:T(8,128)(2,1)S(1)}, u32[]{:S(2)}, u32[]{:S(2)}) collective-permute-start(bf16[2,2,2,2,1,72,256]{6,5,4,3,2,1,0:T(8,128)(2,1)S(1)} %copy-done.57), channel_id=1, source_target_pairs={{0,1},{1,0},{2,3},{3,2},{4,5},{5,4},{6,7},{7,6},{8,9},{9,8},{10,11... | collective-permute-start | bytes 1769480 | tf_op jit(solution)/shard_map/ppermute | solution.py:253
  332.5 112.5 %collective-permute-start.25 = (bf16[2,2,2,2,1,72,256]{6,5,4,3,2,1,0:T(8,128)(2,1)S(1)}, bf16[2,2,2,2,1,72,256]{6,5,4,3,2,1,0:T(8,128)(2,1)S(1)}, u32[]{:S(2)}, u32[]{:S(2)}) collective-permute-start(bf16[2,2,2,2,1,72,256]{6,5,4,3,2,1,0:T(8,128)(2,1)S(1)} %copy-done.56), channel_id=1, source_target_pairs={{0,1},{1,0},{2,3},{3,2},{4,5},{5,4},{6,7},{7,6},{8,9},{9,8},{10,11... | collective-permute-start | bytes 1769480 | tf_op jit(solution)/shard_map/ppermute | solution.py:253
  442.8 9.9 %collective-permute-start.56 = (bf16[2,2,2,1,1,72,256]{6,5,4,3,2,1,0:T(8,128)(2,1)S(1)}, bf16[2,2,2,1,1,72,256]{6,5,4,3,2,1,0:T(8,128)(2,1)S(1)}, u32[]{:S(2)}, u32[]{:S(2)}) collective-permute-start(bf16[2,2,2,1,1,72,256]{6,5,4,3,2,1,0:T(8,128)(2,1)S(1)} %dynamic-slice_convert_fusion.11), channel_id=1, source_target_pairs={{0,2},{1,3},{2,0},{3,1},{4,6},{5,7},{6,4},{7,5},{8,10},{9,11},{10,... | collective-permute-start | bytes 884744 | tf_op jit(solution)/shard_map/ppermute | solution.py:253
  444.4 10.0 %collective-permute-start.61 = (bf16[2,2,1,2,1,72,256]{6,5,4,3,2,1,0:T(8,128)(2,1)S(1)}, bf16[2,2,1,2,1,72,256]{6,5,4,3,2,1,0:T(8,128)(2,1)S(1)}, u32[]{:S(2)}, u32[]{:S(2)}) collective-permute-start(bf16[2,2,1,2,1,72,256]{6,5,4,3,2,1,0:T(8,128)(2,1)S(1)} %dynamic-slice_convert_fusion.10), channel_id=1, source_target_pairs={{0,4},{1,5},{2,6},{3,7},{4,0},{5,1},{6,2},{7,3},{8,12},{9,13},{10,... | collective-permute-start | bytes 884744 | tf_op jit(solution)/shard_map/ppermute | solution.py:253
  444.9 9.8 %collective-permute-start.66 = (bf16[2,1,2,2,1,72,256]{6,5,4,3,2,1,0:T(8,128)(2,1)S(1)}, bf16[2,1,2,2,1,72,256]{6,5,4,3,2,1,0:T(8,128)(2,1)S(1)}, u32[]{:S(2)}, u32[]{:S(2)}) collective-permute-start(bf16[2,1,2,2,1,72,256]{6,5,4,3,2,1,0:T(8,128)(2,1)S(1)} %dynamic-slice_convert_fusion.9), channel_id=1, source_target_pairs={{0,8},{1,9},{2,10},{3,11},{4,12},{5,13},{6,14},{7,15},{8,0},{9,1},... | collective-permute-start | bytes 884744 | tf_op jit(solution)/shard_map/ppermute | solution.py:253
  445.4 12.8 %collective-permute-start.26 = (bf16[2,2,2,1,1,72,256]{6,5,4,3,2,1,0:T(8,128)(2,1)S(1)}, bf16[2,2,2,1,1,72,256]{6,5,4,3,2,1,0:T(8,128)(2,1)S(1)}, u32[]{:S(2)}, u32[]{:S(2)}) collective-permute-start(bf16[2,2,2,1,1,72,256]{6,5,4,3,2,1,0:T(8,128)(2,1)S(1)} %dynamic-slice_convert_fusion.14), channel_id=1, source_target_pairs={{0,2},{1,3},{2,0},{3,1},{4,6},{5,7},{6,4},{7,5},{8,10},{9,11},{10,... | collective-permute-start | bytes 884744 | tf_op jit(solution)/shard_map/ppermute | solution.py:253
  446.4 14.3 %collective-permute-start.31 = (bf16[2,2,1,2,1,72,256]{6,5,4,3,2,1,0:T(8,128)(2,1)S(1)}, bf16[2,2,1,2,1,72,256]{6,5,4,3,2,1,0:T(8,128)(2,1)S(1)}, u32[]{:S(2)}, u32[]{:S(2)}) collective-permute-start(bf16[2,2,1,2,1,72,256]{6,5,4,3,2,1,0:T(8,128)(2,1)S(1)} %dynamic-slice_convert_fusion.13), channel_id=1, source_target_pairs={{0,4},{1,5},{2,6},{3,7},{4,0},{5,1},{6,2},{7,3},{8,12},{9,13},{10,... | collective-permute-start | bytes 884744 | tf_op jit(solution)/shard_map/ppermute | solution.py:253
  454.7 9.9 %collective-permute-start.62 = (bf16[2,1,1,2,1,72,256]{6,5,4,3,2,1,0:T(8,128)(2,1)S(1)}, bf16[2,1,1,2,1,72,256]{6,5,4,3,2,1,0:T(8,128)(2,1)S(1)}, u32[]{:S(2)}, u32[]{:S(2)}) collective-permute-start(bf16[2,1,1,2,1,72,256]{6,5,4,3,2,1,0:T(8,128)(2,1)S(1)} %dynamic-slice_convert_fusion.22), channel_id=1, source_target_pairs={{0,8},{1,9},{2,10},{3,11},{4,12},{5,13},{6,14},{7,15},{8,0},{9,1},... | collective-permute-start | bytes 442376 | tf_op jit(solution)/shard_map/ppermute | solution.py:253
  (137 other events, 1372.2 us)
